TPU v7x, 32 devices: a whole 2x2x4 slice. The times are simulated.
32 devices in a mesh: groups: 2 (over y), graph: 16 (over z, x, core).
Axes of the slice: x: 2, y: 2, z: 4, core: 2. Of those that a mesh axis runs over, the one named last changes fastest.
Arguments:
- edge_state: bfloat16 [8192, 512], P(('groups', 'graph')), parts along dimension 0, may hold values from -6 to 6
- atom_state: bfloat16 [512, 256], P(('groups', 'graph')), parts along dimension 0, may hold values from -6 to 6
- atom_sends: int32 [4096], P(('groups', 'graph')), parts along dimension 0, may hold values from 0 to 15
- edge_source: int32 [8192], P(('groups', 'graph')), parts along dimension 0, may hold values from 0 to 127
- edge_target: int32 [8192], P(('groups', 'graph')), parts along dimension 0, may hold values from 0 to 15
- send_edges: int32 [262144], P(('groups', 'graph')), parts along dimension 0, may hold values from 0 to 255
- triplet_in: int32 [262144], P(('groups', 'graph')), parts along dimension 0, may hold values from 0 to 8191, as said below
- triplet_out: int32 [262144], P(('groups', 'graph')), parts along dimension 0, may hold values from 0 to 8191, as said below
- triplet_valid: int32 [262144], P(('groups', 'graph')), parts along dimension 0, may hold values 0 or 1
- triplet_basis: bfloat16 [16, 262144], P(None, ('groups', 'graph')), parts along dimension 1, may hold values from -6 to 6
- return_edges: int32 [262144], P(('groups', 'graph')), parts along dimension 0, may hold values from 0 to 255
- w_edge: bfloat16 [512, 512], replicated, may hold values from -0.25 to 0.25
- w_source: bfloat16 [256, 512], replicated, may hold values from -0.375 to 0.375
- w_down: bfloat16 [512, 64], replicated, may hold values from -0.25 to 0.25
- w_bilinear: bfloat16 [64, 1024], replicated, may hold values from -0.1875 to 0.1875
- w_up: bfloat16 [64, 512], replicated, may hold values from -0.125 to 0.125
- w_residual: bfloat16 [4, 512, 512], replicated, may hold values from -0.25 to 0.25
- w_atom: bfloat16 [512, 256], replicated, may hold values from -0.25 to 0.25
Outputs:
- edge_out: bfloat16 [8192, 512], P(('groups', 'graph')), parts along dimension 0
- atom_out: bfloat16 [512, 256], P(('groups', 'graph')), parts along dimension 0
There are 2 independent parts, one for each index of `groups`. A program takes and returns all parts, laid end to end along the dimension named above; an argument that names none is the same for every part. Nothing has to cross between parts.
Inputs may be any that keep to these rules, and one draw needn't show every extreme that they name: `atom_sends`: entry d * 8 + c of a device's 128 entries is sent to device d. `send_edges`: entry t * 512 + c of a device's 8192 entries is sent to tile t. `triplet_in`: triplet j of a tile reads a received slot in the same aligned block of 512 slots as j. `triplet_out`: slot d * 512 + c of a tile is returned to device d; triplet j of a tile adds to a slot in the same aligned block of 512 slots as j. `return_edges`: entry t * 512 + c of a device's 8192 entries belongs to the slot that tile t returns in place c.
All inputs are finite; a program needn't handle non-finite values. No bound on the sum of `triplet_valid` on one device may be relied on, other than what follows from the above.
Results may differ from a plain program's by a relative error of at most 0.0095.
Values may be sent and summed in bfloat16 or wider, within the bound.
No kernel may reach another device: no remote copies, remote signals or barrier semaphores. Data moves between devices by JAX's collectives and lax.ppermute only.
A program may use at most 64 MiB of HBM per device.

v0:
```python
import jax
import jax.numpy as jnp
from jax import lax
from jax.sharding import PartitionSpec as P

WIN = 512


inv_root = 0.7071067811865476


def matmul(left, right):
    return jnp.dot(left, right, preferred_element_type=jnp.float32)


def pick_rows(indices, table):
    chooser = (indices[:, None] == jnp.arange(table.shape[0], dtype=jnp.int32)[None, :]).astype(
        table.dtype
    )
    return matmul(chooser, table).astype(table.dtype)


def bilinear_terms(inputs_x, coeffs, keeps, w_bilinear):
    expanded = matmul(inputs_x, w_bilinear)
    expanded = expanded.reshape(inputs_x.shape[0], coeffs.shape[0], -1)
    mixed = jnp.einsum("tkd,kt->td", expanded, coeffs.astype(jnp.float32))
    return mixed * keeps.astype(jnp.float32)[:, None]


def tile_sums(slot_rows, local_in, local_out, keeps, coeffs, w_bilinear):
    trip_count = slot_rows.shape[0]
    block_size = WIN
    block_count = trip_count // block_size
    basis_rows = coeffs.shape[0]
    block_iota = jnp.arange(block_size, dtype=jnp.int32)

    def one_block(operands):
        rows_blk, in_blk, out_blk, keep_blk, coef_blk = operands
        in_hot = ((in_blk % block_size)[:, None] == block_iota[None, :]).astype(jnp.bfloat16)
        inputs_x = matmul(in_hot, rows_blk).astype(jnp.bfloat16)
        mixed = bilinear_terms(inputs_x, coef_blk, keep_blk, w_bilinear)
        out_hot = (block_iota[:, None] == (out_blk % block_size)[None, :]).astype(jnp.float32)
        return jnp.dot(
            out_hot, mixed, precision=lax.Precision.HIGHEST, preferred_element_type=jnp.float32
        )

    shaped_coeffs = jnp.transpose(coeffs.reshape(basis_rows, block_count, block_size), (1, 0, 2))
    summed = lax.map(
        one_block,
        (
            slot_rows.reshape(block_count, block_size, -1),
            local_in.reshape(block_count, block_size),
            local_out.reshape(block_count, block_size),
            keeps.reshape(block_count, block_size),
            shaped_coeffs,
        ),
    )
    return summed.reshape(trip_count, -1).astype(jnp.bfloat16)


def on_device(
    edge_state,
    atom_state,
    atom_sends,
    edge_source,
    edge_target,
    send_edges,
    triplet_in,
    triplet_out,
    triplet_valid,
    triplet_basis,
    return_edges,
    w_edge,
    w_source,
    w_down,
    w_bilinear,
    w_up,
    w_residual,
    w_atom,
):
    edge_count = edge_state.shape[0]
    atom_count = atom_state.shape[0]
    arrived_atoms = lax.all_to_all(
        pick_rows(atom_sends, atom_state), "graph", split_axis=0, concat_axis=0, tiled=True
    )
    src_rows = pick_rows(edge_source, arrived_atoms)
    pre_act = matmul(edge_state, w_edge) + matmul(src_rows, w_source)
    activated = jax.nn.silu(pre_act).astype(jnp.bfloat16)
    projected = jax.nn.silu(matmul(activated, w_down)).astype(jnp.bfloat16)
    slot_rows = lax.all_to_all(
        pick_rows(send_edges, projected), "graph", split_axis=0, concat_axis=0, tiled=True
    )
    slot_sums = tile_sums(
        slot_rows, triplet_in, triplet_out, triplet_valid, triplet_basis, w_bilinear
    )
    returned = lax.all_to_all(slot_sums, "graph", split_axis=0, concat_axis=0, tiled=True)
    back_hot = (jnp.arange(edge_count, dtype=jnp.int32)[:, None] == return_edges[None, :]).astype(
        jnp.bfloat16
    )
    aggregate = matmul(back_hot, returned)
    update = jax.nn.silu(matmul(aggregate.astype(jnp.bfloat16), w_up))
    base = ((edge_state.astype(jnp.float32) + activated.astype(jnp.float32)) * inv_root).astype(
        jnp.bfloat16
    )
    inner_one = jax.nn.silu(matmul(base, w_residual[0])).astype(jnp.bfloat16)
    middle = (
        (base.astype(jnp.float32) + jax.nn.silu(matmul(inner_one, w_residual[1]))) * inv_root
    ).astype(jnp.bfloat16)
    inner_two = jax.nn.silu(matmul(middle, w_residual[2])).astype(jnp.bfloat16)
    chain = (middle.astype(jnp.float32) + jax.nn.silu(matmul(inner_two, w_residual[3]))) * inv_root
    edge_out = (chain + update).astype(jnp.bfloat16)
    contrib = matmul(edge_out, w_atom).astype(jnp.bfloat16)
    one_hot = (edge_target[None, :] == jnp.arange(atom_count, dtype=jnp.int32)[:, None]).astype(
        jnp.bfloat16
    )
    atom_sum = matmul(one_hot, contrib)
    atom_out = (atom_state.astype(jnp.float32) + jax.nn.silu(0.25 * atom_sum)).astype(jnp.bfloat16)
    return (edge_out, atom_out)


def solution(mesh):
    placed = (
        P(("groups", "graph"), None),
        P(("groups", "graph"), None),
        P(("groups", "graph")),
        P(("groups", "graph")),
        P(("groups", "graph")),
        P(("groups", "graph")),
        P(("groups", "graph")),
        P(("groups", "graph")),
        P(("groups", "graph")),
        P(None, ("groups", "graph")),
        P(("groups", "graph")),
        P(),
        P(),
        P(),
        P(),
        P(),
        P(),
        P(),
    )
    return jax.shard_map(
        on_device,
        mesh=mesh,
        in_specs=placed,
        out_specs=(P(("groups", "graph"), None), P(("groups", "graph"), None)),
        check_vma=False,
    )
```

profile of v0, /device:TPU:0, one launch (start us, length us, event | category | flops | bytes accessed | tf_op | source)
XLA Modules:
  0.0 138.8 jit_solution(2237447407892621800)
XLA Ops:
  0.6 1.6 %fusion.21 = bf16[16,8,256]{2,1,0:T(8,128)(2,1)} fusion(bf16[16,256]{1,0:T(8,128)(2,1)} %param.21, s32[128]{0:T(128)} %param.22), kind=kOutput, calls=%fused_computation.37 | convolution fusion | flops 1083392 | bytes 74240 | tf_op jit(solution)/shard_map/dot_general | solution.py:13
  2.3 7.5 %all-to-all-start = ((bf16[16,8,256]{2,1,0:T(8,128)(2,1)}), bf16[16,8,256]{2,1,0:T(8,128)(2,1)S(1)}, u32[]{:S(2)}, u32[]{:S(2)}) async-start(bf16[16,8,256]{2,1,0:T(8,128)(2,1)} %fusion.21), calls=%async_computation | async-start | bytes 131072 | tf_op jit(solution)/shard_map/all_to_all | solution.py:83
  9.8 1.2 fusion.67
  11.0 5.6 %all-to-all-done = bf16[16,8,256]{2,1,0:T(8,128)(2,1)S(1)} async-done(((bf16[16,8,256]{2,1,0:T(8,128)(2,1)}), bf16[16,8,256]{2,1,0:T(8,128)(2,1)S(1)}, u32[]{:S(2)}, u32[]{:S(2)}) %all-to-all-start) | async-done | bytes 65568 | tf_op jit(solution)/shard_map/all_to_all | solution.py:83
  16.7 1.4 %multiply_convert_fusion.4 = bf16[256,512]{1,0:T(8,128)(2,1)S(1)} fusion(f32[256,512]{1,0:T(8,128)S(1)} %fusion.67, bf16[256,512]{1,0:T(8,128)(2,1)} %param.32, bf16[16,8,256]{2,1,0:T(8,128)(2,1)S(1)} %all-to-all-done, s32[256]{0:T(256)} %param.23), kind=kOutput, calls=%fused_computation.59 | convolution fusion | flops 84770816 | bytes 1115136 | tf_op jit(solution)/shard_map/dot_general | solution.py:13
  18.1 1.9 %convolution_convert_fusion.1 = bf16[8192,64]{0,1:T(8,128)(2,1)S(1)} fusion(s32[8192]{0:T(1024)S(1)} %copy-done.11, bf16[256,512]{1,0:T(8,128)(2,1)S(1)} %multiply_convert_fusion.4, bf16[512,64]{0,1:T(8,128)(2,1)S(1)} %copy-done.9), kind=kOutput, calls=%fused_computation.26 | convolution fusion | flops 287916032 | bytes 1409024 | tf_op jit(solution)/shard_map/dot_general | solution.py:13
  20.0 1.1 copy.44
  21.2 4.5 %all-to-all-start.1 = ((bf16[16,512,64]{1,2,0:T(8,128)(2,1)}), bf16[16,512,64]{1,2,0:T(8,128)(2,1)}, u32[]{:S(2)}, u32[]{:S(2)}) async-start(bf16[16,512,64]{1,2,0:T(8,128)(2,1)} %bitcast.66), calls=%async_computation.1 | async-start | bytes 2097152 | tf_op jit(solution)/shard_map/all_to_all | solution.py:90
  26.0 22.6 %all-to-all-done.1 = bf16[16,512,64]{1,2,0:T(8,128)(2,1)} async-done(((bf16[16,512,64]{1,2,0:T(8,128)(2,1)}), bf16[16,512,64]{1,2,0:T(8,128)(2,1)}, u32[]{:S(2)}, u32[]{:S(2)}) %all-to-all-start.1) | async-done | bytes 1048608 | tf_op jit(solution)/shard_map/all_to_all | solution.py:90
  48.6 56.3 %while.14 = (s32[]{:T(128)}, bf16[16,512,64]{1,2,0:T(8,128)(2,1)}, s32[16,512]{1,0:T(8,128)S(1)}, s32[16,512]{1,0:T(8,128)S(1)}, bf16[16,512,64]{1,2,0:T(8,128)(...) while((s32[]{:T(128)}, bf16[16,512,64]{1,2,0:T(8,128)(2,1)}, ...), condition=%wide.region_1.2_spmd.clone.clone, body=%wide.region_0.1_spmd.clone.clone.sunk | while | flops 303615488 | bytes 5150841 | solution.py:48
  48.6 1.7 %fusion.88 = f32[512,1024]{0,1:T(8,128)S(1)} fusion(bf16[64,1024]{1,0:T(8,128)(2,1)S(1)} %get-tuple-element.270, s32[512]{0:T(512)S(1)} %add_select_fusion.2, bf16[16,512,64]{1,2,0:T(8,128)(2,1)} %get-tuple-element.269, s32[]{:T(128)S(6)} %copy.50), kind=kOutput, calls=%fused_computation.5.clone.1 | convolution fusion | flops 100958208 | bytes 2295812 | tf_op jit(solution)/shard_map/while/body/eval_jaxpr/dot_general | solution.py:13
  50.3 0.3 multiply_reduce_fusion.2
  50.7 1.4 fusion.89
  52.1 1.7 %fusion.88 = f32[512,1024]{0,1:T(8,128)S(1)} fusion(bf16[64,1024]{1,0:T(8,128)(2,1)S(1)} %get-tuple-element.270, s32[512]{0:T(512)S(1)} %add_select_fusion.2, bf16[16,512,64]{1,2,0:T(8,128)(2,1)} %get-tuple-element.269, s32[]{:T(128)S(6)} %copy.50), kind=kOutput, calls=%fused_computation.5.clone.1 | convolution fusion | flops 100958208 | bytes 2295812 | tf_op jit(solution)/shard_map/while/body/eval_jaxpr/dot_general | solution.py:13
  53.8 0.3 multiply_reduce_fusion.2
  54.2 1.4 fusion.89
  55.7 1.7 %fusion.88 = f32[512,1024]{0,1:T(8,128)S(1)} fusion(bf16[64,1024]{1,0:T(8,128)(2,1)S(1)} %get-tuple-element.270, s32[512]{0:T(512)S(1)} %add_select_fusion.2, bf16[16,512,64]{1,2,0:T(8,128)(2,1)} %get-tuple-element.269, s32[]{:T(128)S(6)} %copy.50), kind=kOutput, calls=%fused_computation.5.clone.1 | convolution fusion | flops 100958208 | bytes 2295812 | tf_op jit(solution)/shard_map/while/body/eval_jaxpr/dot_general | solution.py:13
  57.4 0.3 multiply_reduce_fusion.2
  57.8 1.4 fusion.89
  59.2 1.7 %fusion.88 = f32[512,1024]{0,1:T(8,128)S(1)} fusion(bf16[64,1024]{1,0:T(8,128)(2,1)S(1)} %get-tuple-element.270, s32[512]{0:T(512)S(1)} %add_select_fusion.2, bf16[16,512,64]{1,2,0:T(8,128)(2,1)} %get-tuple-element.269, s32[]{:T(128)S(6)} %copy.50), kind=kOutput, calls=%fused_computation.5.clone.1 | convolution fusion | flops 100958208 | bytes 2295812 | tf_op jit(solution)/shard_map/while/body/eval_jaxpr/dot_general | solution.py:13
  60.9 0.3 multiply_reduce_fusion.2
  61.3 1.4 fusion.89
  62.7 1.7 %fusion.88 = f32[512,1024]{0,1:T(8,128)S(1)} fusion(bf16[64,1024]{1,0:T(8,128)(2,1)S(1)} %get-tuple-element.270, s32[512]{0:T(512)S(1)} %add_select_fusion.2, bf16[16,512,64]{1,2,0:T(8,128)(2,1)} %get-tuple-element.269, s32[]{:T(128)S(6)} %copy.50), kind=kOutput, calls=%fused_computation.5.clone.1 | convolution fusion | flops 100958208 | bytes 2295812 | tf_op jit(solution)/shard_map/while/body/eval_jaxpr/dot_general | solution.py:13
  64.4 0.3 multiply_reduce_fusion.2
  64.8 1.4 fusion.89
  66.2 1.7 %fusion.88 = f32[512,1024]{0,1:T(8,128)S(1)} fusion(bf16[64,1024]{1,0:T(8,128)(2,1)S(1)} %get-tuple-element.270, s32[512]{0:T(512)S(1)} %add_select_fusion.2, bf16[16,512,64]{1,2,0:T(8,128)(2,1)} %get-tuple-element.269, s32[]{:T(128)S(6)} %copy.50), kind=kOutput, calls=%fused_computation.5.clone.1 | convolution fusion | flops 100958208 | bytes 2295812 | tf_op jit(solution)/shard_map/while/body/eval_jaxpr/dot_general | solution.py:13
  67.9 0.3 multiply_reduce_fusion.2
  68.3 1.4 fusion.89
  69.7 1.7 %fusion.88 = f32[512,1024]{0,1:T(8,128)S(1)} fusion(bf16[64,1024]{1,0:T(8,128)(2,1)S(1)} %get-tuple-element.270, s32[512]{0:T(512)S(1)} %add_select_fusion.2, bf16[16,512,64]{1,2,0:T(8,128)(2,1)} %get-tuple-element.269, s32[]{:T(128)S(6)} %copy.50), kind=kOutput, calls=%fused_computation.5.clone.1 | convolution fusion | flops 100958208 | bytes 2295812 | tf_op jit(solution)/shard_map/while/body/eval_jaxpr/dot_general | solution.py:13
  71.4 0.3 multiply_reduce_fusion.2
  71.8 1.4 fusion.89
  73.3 1.7 %fusion.88 = f32[512,1024]{0,1:T(8,128)S(1)} fusion(bf16[64,1024]{1,0:T(8,128)(2,1)S(1)} %get-tuple-element.270, s32[512]{0:T(512)S(1)} %add_select_fusion.2, bf16[16,512,64]{1,2,0:T(8,128)(2,1)} %get-tuple-element.269, s32[]{:T(128)S(6)} %copy.50), kind=kOutput, calls=%fused_computation.5.clone.1 | convolution fusion | flops 100958208 | bytes 2295812 | tf_op jit(solution)/shard_map/while/body/eval_jaxpr/dot_general | solution.py:13
  75.0 0.3 multiply_reduce_fusion.2
  75.4 1.4 fusion.89
  76.8 1.7 %fusion.88 = f32[512,1024]{0,1:T(8,128)S(1)} fusion(bf16[64,1024]{1,0:T(8,128)(2,1)S(1)} %get-tuple-element.270, s32[512]{0:T(512)S(1)} %add_select_fusion.2, bf16[16,512,64]{1,2,0:T(8,128)(2,1)} %get-tuple-element.269, s32[]{:T(128)S(6)} %copy.50), kind=kOutput, calls=%fused_computation.5.clone.1 | convolution fusion | flops 100958208 | bytes 2295812 | tf_op jit(solution)/shard_map/while/body/eval_jaxpr/dot_general | solution.py:13
  78.5 0.3 multiply_reduce_fusion.2
  78.9 1.4 fusion.89
  80.3 1.7 %fusion.88 = f32[512,1024]{0,1:T(8,128)S(1)} fusion(bf16[64,1024]{1,0:T(8,128)(2,1)S(1)} %get-tuple-element.270, s32[512]{0:T(512)S(1)} %add_select_fusion.2, bf16[16,512,64]{1,2,0:T(8,128)(2,1)} %get-tuple-element.269, s32[]{:T(128)S(6)} %copy.50), kind=kOutput, calls=%fused_computation.5.clone.1 | convolution fusion | flops 100958208 | bytes 2295812 | tf_op jit(solution)/shard_map/while/body/eval_jaxpr/dot_general | solution.py:13
  82.0 0.3 multiply_reduce_fusion.2
  82.4 1.4 fusion.89
  83.8 1.7 %fusion.88 = f32[512,1024]{0,1:T(8,128)S(1)} fusion(bf16[64,1024]{1,0:T(8,128)(2,1)S(1)} %get-tuple-element.270, s32[512]{0:T(512)S(1)} %add_select_fusion.2, bf16[16,512,64]{1,2,0:T(8,128)(2,1)} %get-tuple-element.269, s32[]{:T(128)S(6)} %copy.50), kind=kOutput, calls=%fused_computation.5.clone.1 | convolution fusion | flops 100958208 | bytes 2295812 | tf_op jit(solution)/shard_map/while/body/eval_jaxpr/dot_general | solution.py:13
  85.5 0.3 multiply_reduce_fusion.2
  85.9 1.4 fusion.89
  87.4 1.7 %fusion.88 = f32[512,1024]{0,1:T(8,128)S(1)} fusion(bf16[64,1024]{1,0:T(8,128)(2,1)S(1)} %get-tuple-element.270, s32[512]{0:T(512)S(1)} %add_select_fusion.2, bf16[16,512,64]{1,2,0:T(8,128)(2,1)} %get-tuple-element.269, s32[]{:T(128)S(6)} %copy.50), kind=kOutput, calls=%fused_computation.5.clone.1 | convolution fusion | flops 100958208 | bytes 2295812 | tf_op jit(solution)/shard_map/while/body/eval_jaxpr/dot_general | solution.py:13
  89.0 0.3 multiply_reduce_fusion.2
  89.4 1.4 fusion.89
  90.9 1.7 %fusion.88 = f32[512,1024]{0,1:T(8,128)S(1)} fusion(bf16[64,1024]{1,0:T(8,128)(2,1)S(1)} %get-tuple-element.270, s32[512]{0:T(512)S(1)} %add_select_fusion.2, bf16[16,512,64]{1,2,0:T(8,128)(2,1)} %get-tuple-element.269, s32[]{:T(128)S(6)} %copy.50), kind=kOutput, calls=%fused_computation.5.clone.1 | convolution fusion | flops 100958208 | bytes 2295812 | tf_op jit(solution)/shard_map/while/body/eval_jaxpr/dot_general | solution.py:13
  93.0 1.4 fusion.89
  94.4 1.7 %fusion.88 = f32[512,1024]{0,1:T(8,128)S(1)} fusion(bf16[64,1024]{1,0:T(8,128)(2,1)S(1)} %get-tuple-element.270, s32[512]{0:T(512)S(1)} %add_select_fusion.2, bf16[16,512,64]{1,2,0:T(8,128)(2,1)} %get-tuple-element.269, s32[]{:T(128)S(6)} %copy.50), kind=kOutput, calls=%fused_computation.5.clone.1 | convolution fusion | flops 100958208 | bytes 2295812 | tf_op jit(solution)/shard_map/while/body/eval_jaxpr/dot_general | solution.py:13
  96.1 0.3 multiply_reduce_fusion.2
  96.5 1.4 fusion.89
  97.9 1.7 %fusion.88 = f32[512,1024]{0,1:T(8,128)S(1)} fusion(bf16[64,1024]{1,0:T(8,128)(2,1)S(1)} %get-tuple-element.270, s32[512]{0:T(512)S(1)} %add_select_fusion.2, bf16[16,512,64]{1,2,0:T(8,128)(2,1)} %get-tuple-element.269, s32[]{:T(128)S(6)} %copy.50), kind=kOutput, calls=%fused_computation.5.clone.1 | convolution fusion | flops 100958208 | bytes 2295812 | tf_op jit(solution)/shard_map/while/body/eval_jaxpr/dot_general | solution.py:13
  99.6 0.3 multiply_reduce_fusion.2
  100.0 1.4 fusion.89
  101.4 1.7 %fusion.88 = f32[512,1024]{0,1:T(8,128)S(1)} fusion(bf16[64,1024]{1,0:T(8,128)(2,1)S(1)} %get-tuple-element.270, s32[512]{0:T(512)S(1)} %add_select_fusion.2, bf16[16,512,64]{1,2,0:T(8,128)(2,1)} %get-tuple-element.269, s32[]{:T(128)S(6)} %copy.50), kind=kOutput, calls=%fused_computation.5.clone.1 | convolution fusion | flops 100958208 | bytes 2295812 | tf_op jit(solution)/shard_map/while/body/eval_jaxpr/dot_general | solution.py:13
  103.1 0.3 multiply_reduce_fusion.2
  103.5 1.4 fusion.89
  104.9 6.9 %all-to-all-start.2 = ((bf16[16,512,64]{1,2,0:T(8,128)(2,1)}), bf16[16,512,64]{1,2,0:T(8,128)(2,1)S(1)}, u32[]{:S(2)}, u32[]{:S(2)}) async-start(bf16[16,512,64]{1,2,0:T(8,128)(2,1)} %get-tuple-element.119), calls=%async_computation.2 | async-start | bytes 2097152 | tf_op jit(solution)/shard_map/all_to_all | solution.py:96
  111.9 1.9 %multiply_convert_fusion.1 = bf16[256,512]{1,0:T(8,128)(2,1)S(1)} fusion(bf16[4,512,512]{2,1,0:T(8,128)(2,1)} %param.36, bf16[256,512]{1,0:T(8,128)(2,1)S(1)} %multiply_convert_fusion.4, bf16[256,512]{1,0:T(8,128)(2,1)S(1)} %copy-done.2), kind=kOutput, calls=%fused_computation.54 | convolution fusion | flops 271450112 | bytes 2359296 | tf_op jit(solution)/shard_map/dot_general | solution.py:13
  113.8 1.9 %fusion.25 = f32[256,512]{1,0:T(8,128)S(1)} fusion(bf16[4,512,512]{2,1,0:T(8,128)(2,1)} %param.36, bf16[256,512]{1,0:T(8,128)(2,1)S(1)} %multiply_convert_fusion.1), kind=kOutput, calls=%fused_computation.42 | convolution fusion | flops 269090816 | bytes 1835008 | tf_op jit(solution)/shard_map/dot_general | solution.py:13
  115.7 19.1 %all-to-all-done.2 = bf16[16,512,64]{1,2,0:T(8,128)(2,1)S(1)} async-done(((bf16[16,512,64]{1,2,0:T(8,128)(2,1)}), bf16[16,512,64]{1,2,0:T(8,128)(2,1)S(1)}, u32[]{:S(2)}, u32[]{:S(2)}) %all-to-all-start.2) | async-done | bytes 1048608 | tf_op jit(solution)/shard_map/all_to_all | solution.py:96
  134.9 0.8 copy-done.16
  135.8 2.0 %add_convert_fusion = bf16[256,512]{1,0:T(8,128)(2,1)S(1)} fusion(bf16[64,512]{1,0:T(8,128)(2,1)S(1)} %copy-done.10, bf16[8192,64]{0,1:T(8,128)(2,1)S(1)} %bitcast.85, s32[8192]{0:T(1024)S(1)} %copy-done.12, f32[256,512]{1,0:T(8,128)S(1)} %fusion.25, bf16[256,512]{1,0:T(8,128)(2,1)S(1)} %copy-done.16), kind=kOutput, calls=%fused_computation.50 | convolution fusion | flops 289030144 | bytes 2195456 | tf_op jit(solution)/shard_map/dot_general | solution.py:13
  137.8 1.0 add_convert_fusion.1
  (121 shorter events, 3.4 us)
Async XLA Ops:
  0.6 9.1 %copy-start = (bf16[512,512]{1,0:T(8,128)(2,1)S(1)}, bf16[512,512]{1,0:T(8,128)(2,1)}, u32[]{:S(2)}) copy-start(bf16[512,512]{1,0:T(8,128)(2,1)} %param.31) | copy-start | bytes 1572868
  2.3 15.8 %copy-start.9 = (bf16[512,64]{0,1:T(8,128)(2,1)S(1)}, bf16[512,64]{0,1:T(8,128)(2,1)}, u32[]{:S(2)}) copy-start(bf16[512,64]{0,1:T(8,128)(2,1)} %param.33) | copy-start | bytes 196612
  2.3 15.8 %copy-start.11 = (s32[8192]{0:T(1024)S(1)}, s32[8192]{0:T(1024)}, u32[]{:S(2)}) copy-start(s32[8192]{0:T(1024)} %param.25) | copy-start | bytes 98308
  2.3 14.4 %all-to-all-start = ((bf16[16,8,256]{2,1,0:T(8,128)(2,1)}), bf16[16,8,256]{2,1,0:T(8,128)(2,1)S(1)}, u32[]{:S(2)}, u32[]{:S(2)}) async-start(bf16[16,8,256]{2,1,0:T(8,128)(2,1)} %fusion.21), calls=%async_computation | async-start | bytes 131072 | tf_op jit(solution)/shard_map/all_to_all | solution.py:83
  20.0 5.6 %copy-start.4 = (s32[8192]{0:T(1024)S(1)}, s32[8192]{0:T(1024)}, u32[]{:S(2)}) copy-start(s32[8192]{0:T(1024)} %param.27) | copy-start | bytes 98308
  20.0 5.6 %copy-start.5 = (s32[8192]{0:T(1024)S(1)}, s32[8192]{0:T(1024)}, u32[]{:S(2)}) copy-start(s32[8192]{0:T(1024)} %param.26) | copy-start | bytes 98308
  20.0 5.7 %copy-start.3 = (bf16[16,8192]{1,0:T(8,128)(2,1)S(1)}, bf16[16,8192]{1,0:T(8,128)(2,1)}, u32[]{:S(2)}) copy-start(bf16[16,8192]{1,0:T(8,128)(2,1)} %param.29) | copy-start | bytes 786436
  21.1 4.8 %copy-start.6 = (s32[8192]{0:T(1024)S(1)}, s32[8192]{0:T(1024)}, u32[]{:S(2)}) copy-start(s32[8192]{0:T(1024)} %param.28) | copy-start | bytes 98308
  21.1 27.4 %copy-start.1 = (bf16[64,1024]{1,0:T(8,128)(2,1)S(1)}, bf16[64,1024]{1,0:T(8,128)(2,1)}, u32[]{:S(2)}) copy-start(bf16[64,1024]{1,0:T(8,128)(2,1)} %param.34) | copy-start | bytes 393220
  21.2 27.4 %all-to-all-start.1 = ((bf16[16,512,64]{1,2,0:T(8,128)(2,1)}), bf16[16,512,64]{1,2,0:T(8,128)(2,1)}, u32[]{:S(2)}, u32[]{:S(2)}) async-start(bf16[16,512,64]{1,2,0:T(8,128)(2,1)} %bitcast.66), calls=%async_computation.1 | async-start | bytes 2097152 | tf_op jit(solution)/shard_map/all_to_all | solution.py:90
  104.9 7.0 %copy-start.2 = (bf16[256,512]{1,0:T(8,128)(2,1)S(1)}, bf16[256,512]{1,0:T(8,128)(2,1)}, u32[]{:S(2)}) copy-start(bf16[256,512]{1,0:T(8,128)(2,1)} %param.20) | copy-start | bytes 786436
  104.9 29.9 %all-to-all-start.2 = ((bf16[16,512,64]{1,2,0:T(8,128)(2,1)}), bf16[16,512,64]{1,2,0:T(8,128)(2,1)S(1)}, u32[]{:S(2)}, u32[]{:S(2)}) async-start(bf16[16,512,64]{1,2,0:T(8,128)(2,1)} %get-tuple-element.119), calls=%async_computation.2 | async-start | bytes 2097152 | tf_op jit(solution)/shard_map/all_to_all | solution.py:96
  113.8 1.9 %copy-start.15 = (bf16[256,512]{1,0:T(8,128)(2,1)}, bf16[256,512]{1,0:T(8,128)(2,1)S(1)}, u32[]{:S(2)}) copy-start(bf16[256,512]{1,0:T(8,128)(2,1)S(1)} %multiply_convert_fusion.1) | copy-start | bytes 786436
  115.7 19.2 %copy-start.10 = (bf16[64,512]{1,0:T(8,128)(2,1)S(1)}, bf16[64,512]{1,0:T(8,128)(2,1)}, u32[]{:S(2)}) copy-start(bf16[64,512]{1,0:T(8,128)(2,1)} %param.35) | copy-start | bytes 196612
  115.7 19.2 %copy-start.12 = (s32[8192]{0:T(1024)S(1)}, s32[8192]{0:T(1024)}, u32[]{:S(2)}) copy-start(s32[8192]{0:T(1024)} %param.30) | copy-start | bytes 98308
  134.8 1.0 copy-start.16
  135.8 2.0 %copy-start.7 = (bf16[16,256]{1,0:T(8,128)(2,1)S(1)}, bf16[16,256]{1,0:T(8,128)(2,1)}, u32[]{:S(2)}) copy-start(bf16[16,256]{1,0:T(8,128)(2,1)} %param.21) | copy-start | bytes 24580
  135.8 2.0 %copy-start.8 = (bf16[512,256]{1,0:T(8,128)(2,1)S(1)}, bf16[512,256]{1,0:T(8,128)(2,1)}, u32[]{:S(2)}) copy-start(bf16[512,256]{1,0:T(8,128)(2,1)} %param.37) | copy-start | bytes 786436
  135.8 2.0 %copy-start.13 = (s32[256]{0:T(256)S(1)}, s32[256]{0:T(256)}, u32[]{:S(2)}) copy-start(s32[256]{0:T(256)} %param.24) | copy-start | bytes 3076
  137.8 1.0 copy-start.14
where the time goes:
time: 141 us; the launch traced here: 139 us
  matrix products  61.6 us (44%)
  waiting for transfers between devices  47.3 us (34%)
  starting transfers between devices  18.9 us (13%)
  other arithmetic  4.89 us (3%)
  local copies, waits for them, and re-layouts  4.5 us (3%)
    dot_general x24, matrix products, matmul(): return jnp.dot(left, right, preferred_element_type=jnp.float32)  39.5 us
    all_to_all x1, waiting for transfers between devices, on_device(): lax.all_to_all(pick_rows(send_edges, projected), 'graph', split_axis=0, c...  22.6 us
    dot_general x16, matrix products, one_block(): jnp.dot(out_hot, mixed, precision=lax.Precision.HIGHEST, preferred_elemen...  22 us
    all_to_all x1, waiting for transfers between devices, on_device(): lax.all_to_all(slot_sums, 'graph', split_axis=0, concat_axis=0, tiled=True)  19.1 us
    all_to_all x1, starting transfers between devices, on_device(): lax.all_to_all(pick_rows(atom_sends, atom_state), 'graph', split_axis=0,...  7.48 us
    all_to_all x1, starting transfers between devices, on_device(): lax.all_to_all(slot_sums, 'graph', split_axis=0, concat_axis=0, tiled=True)  6.94 us
    all_to_all x1, waiting for transfers between devices, on_device(): lax.all_to_all(pick_rows(atom_sends, atom_state), 'graph', split_axis=0,...  5.63 us
    while x32, other arithmetic  4.49 us
  transfers between devices with their start and end apart: 3, of which 3 were waited for; matrix products, arithmetic and copies ran while one was open for 4% of the time, Pallas kernels for 0%

commit v1 on v0

--- a/solution.py
+++ b/solution.py
@@ -1,9 +1,14 @@
+import functools
+
 import jax
 import jax.numpy as jnp
 from jax import lax
+from jax.experimental import pallas as pl
+from jax.experimental.pallas import tpu as pltpu
 from jax.sharding import PartitionSpec as P
 
 WIN = 512
+LANES = 128
 
 
 inv_root = 0.7071067811865476
@@ -18,6 +23,224 @@
         table.dtype
     )
     return matmul(chooser, table).astype(table.dtype)
+
+
+def silu(v):
+    return (0.5 * v) * (1.0 + jnp.tanh(0.5 * v))
+
+
+def pack_kernel(basis_ref, valid_ref, in_ref, out_ref, atom_ref, sends_ref, send_ref):
+    basis_rows = basis_ref.shape[0]
+    peers = send_ref.shape[0]
+    pieces = valid_ref.shape[0] // peers
+    width = pieces * LANES
+    atom_slots = sends_ref.shape[1]
+    cap_a = atom_slots // peers
+    chooser = (
+        lax.broadcasted_iota(jnp.int32, (atom_ref.shape[0], atom_slots), 0) == sends_ref[...]
+    ).astype(jnp.float32).astype(jnp.bfloat16)
+    rows = lax.dot_general(
+        chooser, atom_ref[...], (((0,), (0,)), ((), ())), preferred_element_type=jnp.float32
+    ).astype(jnp.bfloat16)
+    keeps = valid_ref[...].astype(jnp.float32)
+    half = width // 2
+    local_in = ((in_ref[...] % width) - half).astype(jnp.float32).astype(jnp.bfloat16)
+    local_out = ((out_ref[...] % width) - half).astype(jnp.float32).astype(jnp.bfloat16)
+    for peer in range(peers):
+        parts = []
+        for piece in range(pieces):
+            row = peer * pieces + piece
+            tile = basis_ref[:, row * LANES : (row + 1) * LANES].astype(jnp.float32)
+            parts.append((tile * keeps[row : row + 1, :]).astype(jnp.bfloat16))
+        parts.append(local_in[peer * pieces : (peer + 1) * pieces, :])
+        parts.append(local_out[peer * pieces : (peer + 1) * pieces, :])
+        for first in range(0, atom_ref.shape[1], LANES):
+            parts.append(rows[peer * cap_a : (peer + 1) * cap_a, first : first + LANES])
+        send_ref[peer] = jnp.concatenate(parts, axis=0)
+
+
+def main_kernel(
+    recv_ref,
+    edge_ref,
+    atom_ref,
+    source_ref,
+    target_ref,
+    send_ref,
+    return_ref,
+    w_edge_ref,
+    w_source_ref,
+    w_down_ref,
+    w_bilinear_ref,
+    w_up_ref,
+    w_residual_ref,
+    w_atom_ref,
+    edge_out_ref,
+    atom_out_ref,
+):
+    bf16, f32 = jnp.bfloat16, jnp.float32
+    peers = recv_ref.shape[0]
+    pieces = send_ref.shape[0] // peers
+    width = pieces * LANES
+    edge_count = edge_ref.shape[0]
+    proj_width = w_down_ref.shape[1]
+    basis_rows = w_bilinear_ref.shape[1] // proj_width
+    index_row = basis_rows * pieces
+    atom_row = index_row + 2 * pieces
+    halves = atom_ref.shape[1] // LANES
+    cap_a = (recv_ref.shape[1] - atom_row) // halves
+
+    arrived = jnp.concatenate(
+        [
+            jnp.concatenate(
+                [
+                    recv_ref[s, atom_row + h * cap_a : atom_row + (h + 1) * cap_a, :]
+                    for s in range(peers)
+                ],
+                axis=0,
+            )
+            for h in range(halves)
+        ],
+        axis=1,
+    )
+    source_hot = (
+        lax.broadcasted_iota(jnp.int32, (arrived.shape[0], edge_count), 0) == source_ref[...]
+    ).astype(f32).astype(bf16)
+    src_rows = lax.dot_general(
+        source_hot, arrived, (((0,), (0,)), ((), ())), preferred_element_type=f32
+    ).astype(bf16)
+    edge = edge_ref[...]
+    activated = silu(matmul(edge, w_edge_ref[...]) + matmul(src_rows, w_source_ref[...])).astype(bf16)
+    projected = silu(matmul(activated, w_down_ref[...])).astype(bf16)
+    expanded = lax.dot_general(
+        w_bilinear_ref[...], projected, (((0,), (1,)), ((), ())), preferred_element_type=f32
+    ).astype(bf16)
+
+    edge_iota = lax.broadcasted_iota(jnp.int32, (edge_count, LANES), 0).astype(f32).astype(bf16)
+    upper = lax.broadcasted_iota(jnp.int32, (2 * pieces, LANES), 0) < pieces
+    one, zero = jnp.ones((), bf16), jnp.zeros((), bf16)
+
+    def one_hot(rows):
+        parts = []
+        for piece in range(pieces):
+            spread = jnp.broadcast_to(rows[piece : piece + 1, :], (edge_count, LANES)).astype(bf16)
+            parts.append(jnp.where(spread == edge_iota, one, zero))
+        return jnp.concatenate(parts, axis=1)
+
+    total = jnp.zeros((edge_count, proj_width), f32)
+    for t in range(peers):
+        slots = recv_ref[t, index_row:atom_row, :].astype(f32).astype(jnp.int32) + width // 2
+        lane, row = slots % LANES, slots // LANES
+        found = jnp.zeros(slots.shape, jnp.int32)
+        for r in range(pieces):
+            here = t * pieces + r
+            table = jnp.where(
+                upper,
+                jnp.broadcast_to(send_ref[here : here + 1, :], slots.shape),
+                jnp.broadcast_to(return_ref[here : here + 1, :], slots.shape),
+            )
+            got = jnp.take_along_axis(table, lane, axis=1, mode="promise_in_bounds")
+            found = jnp.where(row == r, got, found)
+        found = found.astype(f32)
+        in_hot = one_hot(found[:pieces])
+        gathered = matmul(expanded, in_hot)
+        mixed = []
+        for piece in range(pieces):
+            coeffs = recv_ref[t, piece * basis_rows : (piece + 1) * basis_rows, :].astype(f32)
+            part = None
+            for k in range(basis_rows):
+                term = (
+                    gathered[k * proj_width : (k + 1) * proj_width, piece * LANES : (piece + 1) * LANES]
+                    * coeffs[k : k + 1, :]
+                )
+                part = term if part is None else part + term
+            mixed.append(part.astype(bf16))
+        total = total + lax.dot_general(
+            one_hot(found[pieces:]),
+            jnp.concatenate(mixed, axis=1),
+            (((1,), (1,)), ((), ())),
+            preferred_element_type=f32,
+        )
+
+    base = ((edge.astype(f32) + activated.astype(f32)) * inv_root).astype(bf16)
+    inner_one = silu(matmul(base, w_residual_ref[0])).astype(bf16)
+    middle = ((base.astype(f32) + silu(matmul(inner_one, w_residual_ref[1]))) * inv_root).astype(bf16)
+    inner_two = silu(matmul(middle, w_residual_ref[2])).astype(bf16)
+    chain = (middle.astype(f32) + silu(matmul(inner_two, w_residual_ref[3]))) * inv_root
+    update = silu(matmul(total.astype(bf16), w_up_ref[...]))
+    edge_out = (chain + update).astype(bf16)
+    edge_out_ref[...] = edge_out
+    contrib = matmul(edge_out, w_atom_ref[...]).astype(bf16)
+    atom_count = atom_ref.shape[0]
+    target_hot = (
+        lax.broadcasted_iota(jnp.int32, (atom_count, edge_count), 0) == target_ref[...]
+    ).astype(f32).astype(bf16)
+    atom_sum = matmul(target_hot, contrib)
+    atom_out_ref[...] = (atom_ref[...].astype(f32) + silu(0.25 * atom_sum)).astype(bf16)
+
+
+def local_blocks(
+    peers,
+    edge_state,
+    atom_state,
+    atom_sends,
+    edge_source,
+    edge_target,
+    send_edges,
+    triplet_in,
+    triplet_out,
+    triplet_valid,
+    triplet_basis,
+    return_edges,
+    w_edge,
+    w_source,
+    w_down,
+    w_bilinear,
+    w_up,
+    w_residual,
+    w_atom,
+):
+    bf16 = jnp.bfloat16
+    pieces = WIN // LANES
+    rows = triplet_basis.shape[0] * pieces + 2 * pieces
+    rows += atom_sends.shape[0] // peers * (atom_state.shape[1] // LANES)
+    by_lanes = lambda array: array.reshape(-1, LANES)
+    packed = pl.pallas_call(
+        pack_kernel,
+        out_shape=jax.ShapeDtypeStruct((peers, rows, LANES), bf16),
+        name="pack",
+    )(
+        triplet_basis,
+        by_lanes(triplet_valid),
+        by_lanes(triplet_in),
+        by_lanes(triplet_out),
+        atom_state,
+        atom_sends[None, :],
+    )
+    received = lax.all_to_all(packed, "graph", split_axis=0, concat_axis=0, tiled=True)
+    return pl.pallas_call(
+        main_kernel,
+        out_shape=(
+            jax.ShapeDtypeStruct(edge_state.shape, bf16),
+            jax.ShapeDtypeStruct(atom_state.shape, bf16),
+        ),
+        compiler_params=pltpu.CompilerParams(vmem_limit_bytes=48 * 1024 * 1024),
+        name="block",
+    )(
+        received,
+        edge_state,
+        atom_state,
+        edge_source[None, :],
+        edge_target[None, :],
+        by_lanes(send_edges),
+        by_lanes(return_edges),
+        w_edge,
+        w_source,
+        w_down,
+        w_bilinear,
+        w_up,
+        w_residual,
+        w_atom,
+    )
 
 
 def bilinear_terms(inputs_x, coeffs, keeps, w_bilinear):
@@ -58,7 +281,7 @@
     return summed.reshape(trip_count, -1).astype(jnp.bfloat16)
 
 
-def on_device(
+def on_tiles(
     edge_state,
     atom_state,
     atom_sends,
@@ -118,6 +341,13 @@
     return (edge_out, atom_out)
 
 
+def on_device(*arguments):
+    peers = lax.axis_size("graph")
+    if arguments[5].shape[0] == peers * WIN:
+        return local_blocks(peers, *arguments)
+    return on_tiles(*arguments)
+
+
 def solution(mesh):
     placed = (
         P(("groups", "graph"), None),

time: 141 us -> 42.5 us (0.30); the launches traced: 139 us -> 41.8 us
  matrix products: 61.6 us -> 0 us
  waiting for transfers between devices: 47.3 us -> 10.7 us
  starting transfers between devices: 18.9 us -> 7.36 us
  Pallas kernels: 0 us -> 11.3 us
  local copies, waits for them, and re-layouts: 4.5 us -> 11.7 us
  other arithmetic: 4.89 us -> 0 us
    dot_general x40 -> x0, matrix products: 61.6 us -> none  [the longest x24 39.5 us: matmul(): return jnp.dot(left, right, preferred_element_type=jnp.float32)]
    all_to_all x3 -> x1, waiting for transfers between devices: 47.3 us -> 10.7 us  [local_blocks(): lax.all_to_all(packed, 'graph', split_axis=0, concat_axis=0, tiled=True)]
    all_to_all x3 -> x1, starting transfers between devices: 18.9 us -> 7.36 us  [local_blocks(): lax.all_to_all(packed, 'graph', split_axis=0, concat_axis=0, tiled=True)]
    pallas_call x0 -> x2, Pallas kernels: none -> 11.3 us  [the longest x1 9.34 us: local_blocks(): pl.pallas_call(main_kernel, out_shape=(jax.ShapeDtypeStruct(edge_state.sh...]
    unnamed x36 -> x25, local copies, waits for them, and re-layouts: 1.15 us -> 11.7 us
    while x32 -> x0, other arithmetic: 4.49 us -> none
    dot_general x16 -> x0, local copies, waits for them, and re-layouts: 1.95 us -> none  [bilinear_terms(): mixed = jnp.einsum('tkd,kt->td', expanded, coeffs.astype(jnp.float32))]
  transfers between devices with their start and end apart: 3 -> 1, of which waited for: 3 -> 1; matrix products, arithmetic and copies ran while one was open for 4% -> 2% of each run, Pallas kernels for 0% -> 0%
where the time goes in v1:
time: 42.5 us; the launch traced here: 41.8 us
  local copies, waits for them, and re-layouts  11.7 us (28%)
  Pallas kernels  11.3 us (27%)
  waiting for transfers between devices  10.7 us (25%)
  starting transfers between devices  7.36 us (17%)
  between operations  0.66 us (2%)
    unnamed x25, local copies, waits for them, and re-layouts  11.7 us
    all_to_all x1, waiting for transfers between devices, local_blocks(): lax.all_to_all(packed, 'graph', split_axis=0, concat_axis=0, tiled=True)  10.7 us
    pallas_call x1, Pallas kernels, local_blocks(): pl.pallas_call(main_kernel, out_shape=(jax.ShapeDtypeStruct(edge_state.sh...  9.34 us
    all_to_all x1, starting transfers between devices, local_blocks(): lax.all_to_all(packed, 'graph', split_axis=0, concat_axis=0, tiled=True)  7.36 us
    pallas_call x1, Pallas kernels, local_blocks(): pl.pallas_call(pack_kernel, out_shape=jax.ShapeDtypeStruct((peers, rows,...  1.94 us
  transfers between devices with their start and end apart: 1, of which 1 were waited for; matrix products, arithmetic and copies ran while one was open for 2% of the time, Pallas kernels for 0%

profile of v1, /device:TPU:0, one launch (start us, length us, event | category | flops | bytes accessed | tf_op | source)
XLA Modules:
  0.0 41.8 jit_solution(8961023429186674259)
XLA Ops:
  0.6 1.9 %pack.1 = bf16[16,88,128]{2,1,0:T(8,128)(2,1)} custom-call(bf16[16,8192]{1,0:T(8,128)(2,1)} %basis_ref.1, s32[64,128]{1,0:T(8,128)} %bitcast.12, s32[64,128]{1,0:T(8,128)} %bitcast.13, s32[64,128]{1,0:T(8,128)} %bitcast.14, bf16[16,256]{1,0:T(8,128)(2,1)} %atom_ref.3, s32[1,128]{1,0:T(1,128)} %bitcast.15), custom_call_target="tpu_custom_call" | custom-call | tf_op jit(solution)/shard_map/pack/pallas_call | solution.py:207
  2.6 7.4 %all-to-all-start = ((bf16[16,88,128]{2,1,0:T(8,128)(2,1)}), bf16[16,88,128]{2,1,0:T(8,128)(2,1)S(1)}, u32[]{:S(2)}, u32[]{:S(2)}) async-start(bf16[16,88,128]{2,1,0:T(8,128)(2,1)} %pack.1), calls=%async_computation | async-start | bytes 720896 | tf_op jit(solution)/shard_map/all_to_all | solution.py:219
  9.9 1.0 %copy.20.w_down_ref = bf16[512,64]{1,0:T(8,128)(2,1)S(1)} copy(bf16[512,64]{0,1:T(8,128)(2,1)} %param.31) | data formatting | bytes 131072 | tf_op args[13]
  10.9 10.7 %all-to-all-done.recv_ref = bf16[16,88,128]{2,1,0:T(8,128)(2,1)S(1)} async-done(((bf16[16,88,128]{2,1,0:T(8,128)(2,1)}), bf16[16,88,128]{2,1,0:T(8,128)(2,1)S(1)}, u32[]{:S(2)}, u32[]{:S(2)}) %all-to-all-start) | async-done | bytes 360480 | tf_op jit(solution)/shard_map/all_to_all | solution.py:219
  21.6 0.0 copy-start
  21.6 1.6 %copy-done = bf16[4,512,512]{2,1,0:T(8,128)(2,1)S(1)} copy-done((bf16[4,512,512]{2,1,0:T(8,128)(2,1)S(1)}, bf16[4,512,512]{2,1,0:T(8,128)(2,1)}, u32[]{:S(2)}) %copy-start) | copy-done | bytes 2097176
  23.2 0.0 copy-start.1
  23.2 1.0 %copy-done.1 = bf16[512,512]{1,0:T(8,128)(2,1)S(1)} copy-done((bf16[512,512]{1,0:T(8,128)(2,1)S(1)}, bf16[512,512]{1,0:T(8,128)(2,1)}, u32[]{:S(2)}) %copy-start.1) | copy-done | bytes 524312
  24.2 0.0 copy-start.2
  24.2 0.9 %copy-done.2 = bf16[256,512]{1,0:T(8,128)(2,1)S(1)} copy-done((bf16[256,512]{1,0:T(8,128)(2,1)S(1)}, bf16[256,512]{1,0:T(8,128)(2,1)}, u32[]{:S(2)}) %copy-start.2) | copy-done | bytes 262168
  25.2 0.0 copy-start.3
  25.2 0.9 %copy-done.3 = bf16[256,512]{1,0:T(8,128)(2,1)S(1)} copy-done((bf16[256,512]{1,0:T(8,128)(2,1)S(1)}, bf16[256,512]{1,0:T(8,128)(2,1)}, u32[]{:S(2)}) %copy-start.3) | copy-done | bytes 262168
  26.1 0.0 copy-start.4
  26.1 0.9 %copy-done.4 = bf16[512,256]{1,0:T(8,128)(2,1)S(1)} copy-done((bf16[512,256]{1,0:T(8,128)(2,1)S(1)}, bf16[512,256]{1,0:T(8,128)(2,1)}, u32[]{:S(2)}) %copy-start.4) | copy-done | bytes 262168
  27.1 0.0 copy-start.5
  27.1 0.9 %copy-done.5 = bf16[64,1024]{1,0:T(8,128)(2,1)S(1)} copy-done((bf16[64,1024]{1,0:T(8,128)(2,1)S(1)}, bf16[64,1024]{1,0:T(8,128)(2,1)}, u32[]{:S(2)}) %copy-start.5) | copy-done | bytes 131096
  28.0 0.0 copy-start.6
  28.0 0.8 %copy-done.6 = bf16[64,512]{1,0:T(8,128)(2,1)S(1)} copy-done((bf16[64,512]{1,0:T(8,128)(2,1)S(1)}, bf16[64,512]{1,0:T(8,128)(2,1)}, u32[]{:S(2)}) %copy-start.6) | copy-done | bytes 65560
  28.8 0.0 copy-start.7
  28.8 0.7 %copy-done.7 = bf16[16,256]{1,0:T(8,128)(2,1)S(1)} copy-done((bf16[16,256]{1,0:T(8,128)(2,1)S(1)}, bf16[16,256]{1,0:T(8,128)(2,1)}, u32[]{:S(2)}) %copy-start.7) | copy-done | bytes 8216
  29.5 0.0 copy-start.8
  29.5 0.8 %copy-done.8 = s32[8192]{0:T(1024)S(1)} copy-done((s32[8192]{0:T(1024)S(1)}, s32[8192]{0:T(1024)}, u32[]{:S(2)}) %copy-start.8) | copy-done | bytes 32792
  30.3 0.0 copy-start.9
  30.3 0.8 %copy-done.9 = s32[8192]{0:T(1024)S(1)} copy-done((s32[8192]{0:T(1024)S(1)}, s32[8192]{0:T(1024)}, u32[]{:S(2)}) %copy-start.9) | copy-done | bytes 32792
  31.1 0.0 copy-start.10
  31.1 0.7 %copy-done.10 = s32[256]{0:T(256)S(1)} copy-done((s32[256]{0:T(256)S(1)}, s32[256]{0:T(256)}, u32[]{:S(2)}) %copy-start.10) | copy-done | bytes 1048
  31.7 0.0 copy-start.11
  31.7 0.7 %copy-done.11 = s32[256]{0:T(256)S(1)} copy-done((s32[256]{0:T(256)S(1)}, s32[256]{0:T(256)}, u32[]{:S(2)}) %copy-start.11) | copy-done | bytes 1048
  32.4 9.3 %block.1 = (bf16[256,512]{1,0:T(8,128)(2,1)}, bf16[16,256]{1,0:T(8,128)(2,1)}) custom-call(bf16[16,88,128]{2,1,0:T(8,128)(2,1)S(1)} %all-to-all-done.recv_ref, bf16[256,512]{1,0:T(8,128)(2,1)S(1)} %copy-done.2, bf16[16,256]{1,0:T(8,128)(2,1)S(1)} %copy-done.7, s32[1,256]{1,0:T(1,128)S(1)} %bitcast.10, s32[1,256]{1,0:T(1,128)S(1)} %bitcast.11, ...), custom_call_target="tpu_custom_call" | custom-call | tf_op jit(solution)/shard_map/block/pallas_call | solution.py:220
Async XLA Ops:
  2.6 19.0 %all-to-all-start = ((bf16[16,88,128]{2,1,0:T(8,128)(2,1)}), bf16[16,88,128]{2,1,0:T(8,128)(2,1)S(1)}, u32[]{:S(2)}, u32[]{:S(2)}) async-start(bf16[16,88,128]{2,1,0:T(8,128)(2,1)} %pack.1), calls=%async_computation | async-start | bytes 720896 | tf_op jit(solution)/shard_map/all_to_all | solution.py:219
  21.6 1.6 %copy-start = (bf16[4,512,512]{2,1,0:T(8,128)(2,1)S(1)}, bf16[4,512,512]{2,1,0:T(8,128)(2,1)}, u32[]{:S(2)}) copy-start(bf16[4,512,512]{2,1,0:T(8,128)(2,1)} %w_residual_ref.1) | copy-start | bytes 6291460
  23.2 1.0 %copy-start.1 = (bf16[512,512]{1,0:T(8,128)(2,1)S(1)}, bf16[512,512]{1,0:T(8,128)(2,1)}, u32[]{:S(2)}) copy-start(bf16[512,512]{1,0:T(8,128)(2,1)} %w_edge_ref.1) | copy-start | bytes 1572868
  24.2 0.9 %copy-start.2 = (bf16[256,512]{1,0:T(8,128)(2,1)S(1)}, bf16[256,512]{1,0:T(8,128)(2,1)}, u32[]{:S(2)}) copy-start(bf16[256,512]{1,0:T(8,128)(2,1)} %edge_ref.1) | copy-start | bytes 786436
  25.2 0.9 %copy-start.3 = (bf16[256,512]{1,0:T(8,128)(2,1)S(1)}, bf16[256,512]{1,0:T(8,128)(2,1)}, u32[]{:S(2)}) copy-start(bf16[256,512]{1,0:T(8,128)(2,1)} %w_source_ref.1) | copy-start | bytes 786436
  26.1 0.9 %copy-start.4 = (bf16[512,256]{1,0:T(8,128)(2,1)S(1)}, bf16[512,256]{1,0:T(8,128)(2,1)}, u32[]{:S(2)}) copy-start(bf16[512,256]{1,0:T(8,128)(2,1)} %w_atom_ref.1) | copy-start | bytes 786436
  27.1 0.9 %copy-start.5 = (bf16[64,1024]{1,0:T(8,128)(2,1)S(1)}, bf16[64,1024]{1,0:T(8,128)(2,1)}, u32[]{:S(2)}) copy-start(bf16[64,1024]{1,0:T(8,128)(2,1)} %w_bilinear_ref.1) | copy-start | bytes 393220
  28.0 0.8 %copy-start.6 = (bf16[64,512]{1,0:T(8,128)(2,1)S(1)}, bf16[64,512]{1,0:T(8,128)(2,1)}, u32[]{:S(2)}) copy-start(bf16[64,512]{1,0:T(8,128)(2,1)} %w_up_ref.1) | copy-start | bytes 196612
  28.8 0.7 %copy-start.7 = (bf16[16,256]{1,0:T(8,128)(2,1)S(1)}, bf16[16,256]{1,0:T(8,128)(2,1)}, u32[]{:S(2)}) copy-start(bf16[16,256]{1,0:T(8,128)(2,1)} %atom_ref.3) | copy-start | bytes 24580
  29.5 0.8 %copy-start.8 = (s32[8192]{0:T(1024)S(1)}, s32[8192]{0:T(1024)}, u32[]{:S(2)}) copy-start(s32[8192]{0:T(1024)} %param.23) | copy-start | bytes 98308
  30.3 0.8 %copy-start.9 = (s32[8192]{0:T(1024)S(1)}, s32[8192]{0:T(1024)}, u32[]{:S(2)}) copy-start(s32[8192]{0:T(1024)} %param.28) | copy-start | bytes 98308
  31.1 0.7 %copy-start.10 = (s32[256]{0:T(256)S(1)}, s32[256]{0:T(256)}, u32[]{:S(2)}) copy-start(s32[256]{0:T(256)} %param.21) | copy-start | bytes 3076
  31.7 0.7 %copy-start.11 = (s32[256]{0:T(256)S(1)}, s32[256]{0:T(256)}, u32[]{:S(2)}) copy-start(s32[256]{0:T(256)} %param.22) | copy-start | bytes 3076

commit v2 on v1

--- a/solution.py
+++ b/solution.py
@@ -59,30 +59,42 @@
         send_ref[peer] = jnp.concatenate(parts, axis=0)
 
 
-def main_kernel(
-    recv_ref,
-    edge_ref,
-    atom_ref,
-    source_ref,
-    target_ref,
-    send_ref,
-    return_ref,
-    w_edge_ref,
-    w_source_ref,
-    w_down_ref,
-    w_bilinear_ref,
-    w_up_ref,
-    w_residual_ref,
-    w_atom_ref,
-    edge_out_ref,
-    atom_out_ref,
-):
+def main_kernel(recv_ref, *refs):
+    count = (len(refs) - 3) // 2
+    far, (edge_out_ref, atom_out_ref) = refs[:count], refs[count : count + 2]
+    near, sems = refs[count + 2 : -1], refs[-1]
+    copies = [
+        pltpu.make_async_copy(here, there, sems.at[at])
+        for at, (here, there) in enumerate(zip(far, near))
+    ]
+    for copy in copies:
+        copy.start()
+    (
+        edge_ref,
+        w_edge_ref,
+        source_ref,
+        atom_ref,
+        w_source_ref,
+        w_down_t_ref,
+        w_bilinear_ref,
+        send_ref,
+        return_ref,
+        w_residual_ref,
+        w_up_ref,
+        w_atom_ref,
+        target_ref,
+    ) = near
+
+    def ready(*ats):
+        for at in ats:
+            copies[at].wait()
+
     bf16, f32 = jnp.bfloat16, jnp.float32
     peers = recv_ref.shape[0]
     pieces = send_ref.shape[0] // peers
     width = pieces * LANES
     edge_count = edge_ref.shape[0]
-    proj_width = w_down_ref.shape[1]
+    proj_width = w_down_t_ref.shape[0]
     basis_rows = w_bilinear_ref.shape[1] // proj_width
     index_row = basis_rows * pieces
     atom_row = index_row + 2 * pieces
@@ -102,19 +114,27 @@
         ],
         axis=1,
     )
+    ready(2)
     source_hot = (
         lax.broadcasted_iota(jnp.int32, (arrived.shape[0], edge_count), 0) == source_ref[...]
     ).astype(f32).astype(bf16)
     src_rows = lax.dot_general(
         source_hot, arrived, (((0,), (0,)), ((), ())), preferred_element_type=f32
     ).astype(bf16)
+    ready(0, 1, 3, 4)
     edge = edge_ref[...]
     activated = silu(matmul(edge, w_edge_ref[...]) + matmul(src_rows, w_source_ref[...])).astype(bf16)
-    projected = silu(matmul(activated, w_down_ref[...])).astype(bf16)
+    ready(5, 6)
+    projected = silu(
+        lax.dot_general(
+            activated, w_down_t_ref[...], (((1,), (1,)), ((), ())), preferred_element_type=f32
+        )
+    ).astype(bf16)
     expanded = lax.dot_general(
         w_bilinear_ref[...], projected, (((0,), (1,)), ((), ())), preferred_element_type=f32
     ).astype(bf16)
 
+    ready(7, 8)
     edge_iota = lax.broadcasted_iota(jnp.int32, (edge_count, LANES), 0).astype(f32).astype(bf16)
     upper = lax.broadcasted_iota(jnp.int32, (2 * pieces, LANES), 0) < pieces
     one, zero = jnp.ones((), bf16), jnp.zeros((), bf16)
@@ -161,6 +181,7 @@
             preferred_element_type=f32,
         )
 
+    ready(9, 10, 11, 12)
     base = ((edge.astype(f32) + activated.astype(f32)) * inv_root).astype(bf16)
     inner_one = silu(matmul(base, w_residual_ref[0])).astype(bf16)
     middle = ((base.astype(f32) + silu(matmul(inner_one, w_residual_ref[1]))) * inv_root).astype(bf16)
@@ -217,30 +238,32 @@
         atom_sends[None, :],
     )
     received = lax.all_to_all(packed, "graph", split_axis=0, concat_axis=0, tiled=True)
+    operands = (
+        edge_state,
+        w_edge,
+        edge_source[None, :],
+        atom_state,
+        w_source,
+        w_down.T,
+        w_bilinear,
+        by_lanes(send_edges),
+        by_lanes(return_edges),
+        w_residual,
+        w_up,
+        w_atom,
+        edge_target[None, :],
+    )
+    like = lambda array: jax.ShapeDtypeStruct(array.shape, array.dtype)
     return pl.pallas_call(
         main_kernel,
-        out_shape=(
-            jax.ShapeDtypeStruct(edge_state.shape, bf16),
-            jax.ShapeDtypeStruct(atom_state.shape, bf16),
-        ),
-        compiler_params=pltpu.CompilerParams(vmem_limit_bytes=48 * 1024 * 1024),
+        in_specs=[pl.BlockSpec(memory_space=pltpu.VMEM)]
+        + [pl.BlockSpec(memory_space=pltpu.HBM)] * len(operands),
+        out_shape=(like(edge_state), like(atom_state)),
+        scratch_shapes=[pltpu.VMEM(array.shape, array.dtype) for array in operands]
+        + [pltpu.SemaphoreType.DMA((len(operands),))],
+        compiler_params=pltpu.CompilerParams(vmem_limit_bytes=32 * 1024 * 1024),
         name="block",
-    )(
-        received,
-        edge_state,
-        atom_state,
-        edge_source[None, :],
-        edge_target[None, :],
-        by_lanes(send_edges),
-        by_lanes(return_edges),
-        w_edge,
-        w_source,
-        w_down,
-        w_bilinear,
-        w_up,
-        w_residual,
-        w_atom,
-    )
+    )(received, *(pltpu.with_memory_space_constraint(array, pltpu.HBM) for array in operands))
 
 
 def bilinear_terms(inputs_x, coeffs, keeps, w_bilinear):

time: 42.5 us -> 33.3 us (0.78); the launches traced: 41.8 us -> 33.1 us
  blocking collectives: 0 us -> 19 us
  local copies, waits for them, and re-layouts: 11.7 us -> 0 us
  waiting for transfers between devices: 10.7 us -> 0 us
  starting transfers between devices: 7.36 us -> 0 us
  Pallas kernels: 11.3 us -> 13.4 us
    all_to_all x0 -> x1, blocking collectives: none -> 19 us  [local_blocks(): lax.all_to_all(packed, 'graph', split_axis=0, concat_axis=0, tiled=True)]
    unnamed x25 -> x0, local copies, waits for them, and re-layouts: 11.7 us -> none
    all_to_all x1 -> x0, waiting for transfers between devices: 10.7 us -> none  [local_blocks(): lax.all_to_all(packed, 'graph', split_axis=0, concat_axis=0, tiled=True)]
    all_to_all x1 -> x0, starting transfers between devices: 7.36 us -> none  [local_blocks(): lax.all_to_all(packed, 'graph', split_axis=0, concat_axis=0, tiled=True)]
    pallas_call x1, Pallas kernels: 9.34 us -> 11.5 us  [local_blocks(): pl.pallas_call(main_kernel, in_specs=[pl.BlockSpec(memory_space=pltpu.VME...]
  transfers between devices with their start and end apart: 1 -> 0, of which waited for: 1 -> 0; matrix products, arithmetic and copies ran while one was open for 2% -> 0% of each run, Pallas kernels for 0% -> 0%
where the time goes in v2:
time: 33.3 us; the launch traced here: 33.1 us
  blocking collectives  19 us (57%)
  Pallas kernels  13.4 us (40%)
  between operations  0.63 us (2%)
    all_to_all x1, blocking collectives, local_blocks(): lax.all_to_all(packed, 'graph', split_axis=0, concat_axis=0, tiled=True)  19 us
    pallas_call x1, Pallas kernels, local_blocks(): pl.pallas_call(main_kernel, in_specs=[pl.BlockSpec(memory_space=pltpu.VME...  11.5 us
    pallas_call x1, Pallas kernels, local_blocks(): pl.pallas_call(pack_kernel, out_shape=jax.ShapeDtypeStruct((peers, rows,...  1.93 us

profile of v2, /device:TPU:0, one launch (start us, length us, event | category | flops | bytes accessed | tf_op | source)
XLA Modules:
  0.0 33.1 jit_solution(17078210134531057340)
XLA Ops:
  0.6 1.9 %pack.1 = bf16[16,88,128]{2,1,0:T(8,128)(2,1)} custom-call(bf16[16,8192]{1,0:T(8,128)(2,1)} %basis_ref.1, s32[64,128]{1,0:T(8,128)} %bitcast.12, s32[64,128]{1,0:T(8,128)} %bitcast.13, s32[64,128]{1,0:T(8,128)} %bitcast.14, bf16[16,256]{1,0:T(8,128)(2,1)} %refs_3_.1, s32[1,128]{1,0:T(1,128)} %bitcast.17), custom_call_target="tpu_custom_call" | custom-call | tf_op jit(solution)/shard_map/pack/pallas_call | solution.py:228
  2.6 19.0 %all_to_all.5.recv_ref = bf16[16,88,128]{2,1,0:T(8,128)(2,1)S(1)} all-to-all(bf16[16,88,128]{2,1,0:T(8,128)(2,1)} %pack.1), channel_id=1, replica_groups=mesh['groups'=2,'graph'=16] {'graph'}, dimensions={0} | all-to-all | bytes 720896 | tf_op jit(solution)/shard_map/all_to_all | solution.py:240
  21.6 11.5 %block.1 = (bf16[256,512]{1,0:T(8,128)(2,1)}, bf16[16,256]{1,0:T(8,128)(2,1)}) custom-call(bf16[16,88,128]{2,1,0:T(8,128)(2,1)S(1)} %all_to_all.5.recv_ref, bf16[256,512]{1,0:T(8,128)(2,1)} %refs_0_.1, bf16[512,512]{1,0:T(8,128)(2,1)} %refs_1_.1, s32[1,256]{1,0:T(1,128)} %bitcast.15, bf16[16,256]{1,0:T(8,128)(2,1)} %refs_3_.1, bf16[256,512]{1,0:T(8,128)(2,1)} %refs_4_.1, ...), custom_call_target="tpu_custom_call" | custom-call | tf_op jit(solution)/shard_map/block/pallas_call | solution.py:257

commit v3 on v2

--- a/solution.py
+++ b/solution.py
@@ -1,5 +1,3 @@
-import functools
-
 import jax
 import jax.numpy as jnp
 from jax import lax
@@ -59,7 +57,57 @@
         send_ref[peer] = jnp.concatenate(parts, axis=0)
 
 
-def main_kernel(recv_ref, *refs):
+def ahead_kernel(
+    edge_far,
+    w_edge_far,
+    source_far,
+    w_bilinear_far,
+    w_source_far,
+    w_down_t_far,
+    edge_ref,
+    pre_ref,
+    source_hot_ref,
+    w_bilinear_t_ref,
+    w_source_ref,
+    w_down_t_ref,
+    w_edge_ref,
+    source_ref,
+    w_bilinear_ref,
+    sems,
+):
+    copies = [
+        pltpu.make_async_copy(here, there, sems.at[at])
+        for at, (here, there) in enumerate(
+            (
+                (edge_far, edge_ref),
+                (w_edge_far, w_edge_ref),
+                (source_far, source_ref),
+                (w_bilinear_far, w_bilinear_ref),
+                (w_source_far, w_source_ref),
+                (w_down_t_far, w_down_t_ref),
+            )
+        )
+    ]
+    for copy in copies:
+        copy.start()
+    for copy in copies:
+        copy.wait()
+    pre_ref[...] = matmul(edge_ref[...], w_edge_ref[...])
+    w_bilinear_t_ref[...] = w_bilinear_ref[...].T
+    hot = lax.broadcasted_iota(jnp.int32, source_hot_ref.shape[::-1], 0) == source_ref[...]
+    source_hot_ref[...] = hot.astype(jnp.float32).T.astype(jnp.bfloat16)
+
+
+def main_kernel(
+    recv_ref,
+    edge_ref,
+    pre_ref,
+    source_hot_ref,
+    w_bilinear_t_ref,
+    w_source_ref,
+    w_down_t_ref,
+    *refs,
+):
     count = (len(refs) - 3) // 2
     far, (edge_out_ref, atom_out_ref) = refs[:count], refs[count : count + 2]
     near, sems = refs[count + 2 : -1], refs[-1]
@@ -69,21 +117,7 @@
     ]
     for copy in copies:
         copy.start()
-    (
-        edge_ref,
-        w_edge_ref,
-        source_ref,
-        atom_ref,
-        w_source_ref,
-        w_down_t_ref,
-        w_bilinear_ref,
-        send_ref,
-        return_ref,
-        w_residual_ref,
-        w_up_ref,
-        w_atom_ref,
-        target_ref,
-    ) = near
+    send_ref, return_ref, w_residual_ref, w_up_ref, w_atom_ref, target_ref, atom_ref = near
 
     def ready(*ats):
         for at in ats:
@@ -95,10 +129,10 @@
     width = pieces * LANES
     edge_count = edge_ref.shape[0]
     proj_width = w_down_t_ref.shape[0]
-    basis_rows = w_bilinear_ref.shape[1] // proj_width
+    basis_rows = w_bilinear_t_ref.shape[0] // proj_width
     index_row = basis_rows * pieces
     atom_row = index_row + 2 * pieces
-    halves = atom_ref.shape[1] // LANES
+    halves = atom_out_ref.shape[1] // LANES
     cap_a = (recv_ref.shape[1] - atom_row) // halves
 
     arrived = jnp.concatenate(
@@ -114,27 +148,19 @@
         ],
         axis=1,
     )
-    ready(2)
-    source_hot = (
-        lax.broadcasted_iota(jnp.int32, (arrived.shape[0], edge_count), 0) == source_ref[...]
-    ).astype(f32).astype(bf16)
-    src_rows = lax.dot_general(
-        source_hot, arrived, (((0,), (0,)), ((), ())), preferred_element_type=f32
-    ).astype(bf16)
-    ready(0, 1, 3, 4)
+    src_rows = matmul(source_hot_ref[...], arrived).astype(bf16)
     edge = edge_ref[...]
-    activated = silu(matmul(edge, w_edge_ref[...]) + matmul(src_rows, w_source_ref[...])).astype(bf16)
-    ready(5, 6)
+    activated = silu(pre_ref[...] + matmul(src_rows, w_source_ref[...])).astype(bf16)
     projected = silu(
         lax.dot_general(
             activated, w_down_t_ref[...], (((1,), (1,)), ((), ())), preferred_element_type=f32
         )
     ).astype(bf16)
     expanded = lax.dot_general(
-        w_bilinear_ref[...], projected, (((0,), (1,)), ((), ())), preferred_element_type=f32
+        w_bilinear_t_ref[...], projected, (((1,), (1,)), ((), ())), preferred_element_type=f32
     ).astype(bf16)
 
-    ready(7, 8)
+    ready(0, 1)
     edge_iota = lax.broadcasted_iota(jnp.int32, (edge_count, LANES), 0).astype(f32).astype(bf16)
     upper = lax.broadcasted_iota(jnp.int32, (2 * pieces, LANES), 0) < pieces
     one, zero = jnp.ones((), bf16), jnp.zeros((), bf16)
@@ -181,7 +207,7 @@
             preferred_element_type=f32,
         )
 
-    ready(9, 10, 11, 12)
+    ready(2, 3, 4, 5, 6)
     base = ((edge.astype(f32) + activated.astype(f32)) * inv_root).astype(bf16)
     inner_one = silu(matmul(base, w_residual_ref[0])).astype(bf16)
     middle = ((base.astype(f32) + silu(matmul(inner_one, w_residual_ref[1]))) * inv_root).astype(bf16)
@@ -238,32 +264,47 @@
         atom_sends[None, :],
     )
     received = lax.all_to_all(packed, "graph", split_axis=0, concat_axis=0, tiled=True)
-    operands = (
-        edge_state,
-        w_edge,
-        edge_source[None, :],
-        atom_state,
-        w_source,
-        w_down.T,
-        w_bilinear,
+    like = lambda array: jax.ShapeDtypeStruct(array.shape, array.dtype)
+    stay = lambda arrays: [pltpu.with_memory_space_constraint(one, pltpu.HBM) for one in arrays]
+    near, far = pl.BlockSpec(memory_space=pltpu.VMEM), pl.BlockSpec(memory_space=pltpu.HBM)
+    source, w_down_t = edge_source[None, :], w_down.T
+    early = pl.pallas_call(
+        ahead_kernel,
+        in_specs=[far] * 6,
+        out_specs=[near] * 6,
+        out_shape=(
+            like(edge_state),
+            jax.ShapeDtypeStruct((edge_state.shape[0], w_edge.shape[1]), jnp.float32),
+            jax.ShapeDtypeStruct((edge_state.shape[0], atom_sends.shape[0]), bf16),
+            jax.ShapeDtypeStruct(w_bilinear.shape[::-1], bf16),
+            like(w_source),
+            like(w_down_t),
+        ),
+        scratch_shapes=[
+            pltpu.VMEM(array.shape, array.dtype) for array in (w_edge, source, w_bilinear)
+        ]
+        + [pltpu.SemaphoreType.DMA((6,))],
+        compiler_params=pltpu.CompilerParams(vmem_limit_bytes=8 * 1024 * 1024),
+        name="ahead",
+    )(*stay((edge_state, w_edge, source, w_bilinear, w_source, w_down_t)))
+    late = (
         by_lanes(send_edges),
         by_lanes(return_edges),
         w_residual,
         w_up,
         w_atom,
         edge_target[None, :],
-    )
-    like = lambda array: jax.ShapeDtypeStruct(array.shape, array.dtype)
+        atom_state,
+    )
     return pl.pallas_call(
         main_kernel,
-        in_specs=[pl.BlockSpec(memory_space=pltpu.VMEM)]
-        + [pl.BlockSpec(memory_space=pltpu.HBM)] * len(operands),
+        in_specs=[near] * 7 + [far] * len(late),
         out_shape=(like(edge_state), like(atom_state)),
-        scratch_shapes=[pltpu.VMEM(array.shape, array.dtype) for array in operands]
-        + [pltpu.SemaphoreType.DMA((len(operands),))],
+        scratch_shapes=[pltpu.VMEM(array.shape, array.dtype) for array in late]
+        + [pltpu.SemaphoreType.DMA((len(late),))],
         compiler_params=pltpu.CompilerParams(vmem_limit_bytes=32 * 1024 * 1024),
         name="block",
-    )(received, *(pltpu.with_memory_space_constraint(array, pltpu.HBM) for array in operands))
+    )(received, *early, *stay(late))
 
 
 def bilinear_terms(inputs_x, coeffs, keeps, w_bilinear):

time: 33.3 us -> 32.6 us (0.979)
  blocking collectives: 19 us -> 0 us
  waiting for transfers between devices: 0 us -> 10.1 us
  starting transfers between devices: 0 us -> 7.36 us
  Pallas kernels: 13.4 us -> 14.3 us
    all_to_all x1 -> x0, blocking collectives: 19 us -> none  [local_blocks(): lax.all_to_all(packed, 'graph', split_axis=0, concat_axis=0, tiled=True)]
    all_to_all x0 -> x1, waiting for transfers between devices: none -> 10.1 us  [local_blocks(): lax.all_to_all(packed, 'graph', split_axis=0, concat_axis=0, tiled=True)]
    all_to_all x0 -> x1, starting transfers between devices: none -> 7.36 us  [local_blocks(): lax.all_to_all(packed, 'graph', split_axis=0, concat_axis=0, tiled=True)]
    pallas_call x1 -> x2, Pallas kernels: 11.5 us -> 12.3 us  [the longest x1 10.7 us: local_blocks(): pl.pallas_call(main_kernel, in_specs=[near] * 7 + [far] * len(late), out_...]
  transfers between devices with their start and end apart: 0 -> 1, of which waited for: 0 -> 1; matrix products, arithmetic and copies ran while one was open for 0% -> 0% of each run, Pallas kernels for 0% -> 5%
where the time goes in v3:
time: 32.6 us; the launch traced here: 32.3 us
  Pallas kernels  14.3 us (44%)
  waiting for transfers between devices  10.1 us (31%)
  starting transfers between devices  7.36 us (23%)
  between operations  0.65 us (2%)
    pallas_call x1, Pallas kernels, local_blocks(): pl.pallas_call(main_kernel, in_specs=[near] * 7 + [far] * len(late), out_...  10.7 us
    all_to_all x1, waiting for transfers between devices, local_blocks(): lax.all_to_all(packed, 'graph', split_axis=0, concat_axis=0, tiled=True)  10.1 us
    all_to_all x1, starting transfers between devices, local_blocks(): lax.all_to_all(packed, 'graph', split_axis=0, concat_axis=0, tiled=True)  7.36 us
    pallas_call x1, Pallas kernels, local_blocks(): pl.pallas_call(pack_kernel, out_shape=jax.ShapeDtypeStruct((peers, rows,...  1.93 us
    pallas_call x1, Pallas kernels, local_blocks(): pl.pallas_call(ahead_kernel, in_specs=[far] * 6, out_specs=[near] * 6, ou...  1.61 us
  transfers between devices with their start and end apart: 1, of which 1 were waited for; matrix products, arithmetic and copies ran while one was open for 0% of the time, Pallas kernels for 5%

profile of v3, /device:TPU:0, one launch (start us, length us, event | category | flops | bytes accessed | tf_op | source)
XLA Modules:
  0.0 32.3 jit_solution(2097756850252038951)
XLA Ops:
  0.6 1.9 %pack.1 = bf16[16,88,128]{2,1,0:T(8,128)(2,1)} custom-call(bf16[16,8192]{1,0:T(8,128)(2,1)} %basis_ref.1, s32[64,128]{1,0:T(8,128)} %bitcast.12, s32[64,128]{1,0:T(8,128)} %bitcast.13, s32[64,128]{1,0:T(8,128)} %bitcast.14, bf16[16,256]{1,0:T(8,128)(2,1)} %refs_6_.1, s32[1,128]{1,0:T(1,128)} %bitcast.17), custom_call_target="tpu_custom_call" | custom-call | tf_op jit(solution)/shard_map/pack/pallas_call | solution.py:254
  2.6 7.4 %all-to-all-start = ((bf16[16,88,128]{2,1,0:T(8,128)(2,1)}), bf16[16,88,128]{2,1,0:T(8,128)(2,1)S(1)}, u32[]{:S(2)}, u32[]{:S(2)}) async-start(bf16[16,88,128]{2,1,0:T(8,128)(2,1)} %pack.1), calls=%async_computation | async-start | bytes 720896 | tf_op jit(solution)/shard_map/all_to_all | solution.py:266
  9.9 1.6 %ahead.1 = (bf16[256,512]{1,0:T(8,128)(2,1)S(1)}, f32[256,512]{1,0:T(8,128)S(1)}, bf16[256,128]{1,0:T(8,128)(2,1)S(1)}, bf16[1024,64]{1,0:T(8,128)(2,1)S(1)}, bf...) custom-call(bf16[256,512]{1,0:T(8,128)(2,1)} %edge_far.1, bf16[512,512]{1,0:T(8,128)(2,1)} %w_edge_far.1, ...), custom_call_target="tpu_custom_call" | custom-call | tf_op jit(solution)/shard_map/ahead/pallas_call | solution.py:271
  11.5 10.1 %all-to-all-done.recv_ref = bf16[16,88,128]{2,1,0:T(8,128)(2,1)S(1)} async-done(((bf16[16,88,128]{2,1,0:T(8,128)(2,1)}), bf16[16,88,128]{2,1,0:T(8,128)(2,1)S(1)}, u32[]{:S(2)}, u32[]{:S(2)}) %all-to-all-start) | async-done | bytes 360480 | tf_op jit(solution)/shard_map/all_to_all | solution.py:266
  21.6 10.7 %block.1 = (bf16[256,512]{1,0:T(8,128)(2,1)}, bf16[16,256]{1,0:T(8,128)(2,1)}) custom-call(bf16[16,88,128]{2,1,0:T(8,128)(2,1)S(1)} %all-to-all-done.recv_ref, bf16[256,512]{1,0:T(8,128)(2,1)S(1)} %get-tuple-element.8.edge_ref, f32[256,512]{1,0:T(8,128)S(1)} %get-tuple-element.9.pre_ref, bf16[256,128]{1,0:T(8,128)(2,1)S(1)} %get-tuple-element.10.source_hot_ref, ...), custom_call_target="tpu_custom_call" | custom-call | tf_op jit(solution)/shard_map/block/pallas_call | solution.py:299
Async XLA Ops:
  2.6 19.0 %all-to-all-start = ((bf16[16,88,128]{2,1,0:T(8,128)(2,1)}), bf16[16,88,128]{2,1,0:T(8,128)(2,1)S(1)}, u32[]{:S(2)}, u32[]{:S(2)}) async-start(bf16[16,88,128]{2,1,0:T(8,128)(2,1)} %pack.1), calls=%async_computation | async-start | bytes 720896 | tf_op jit(solution)/shard_map/all_to_all | solution.py:266

commit v4 on v3

--- a/solution.py
+++ b/solution.py
@@ -62,19 +62,31 @@
     w_edge_far,
     source_far,
     w_bilinear_far,
+    target_far,
+    atom_far,
     w_source_far,
     w_down_t_far,
+    send_far,
+    return_far,
+    w_up_far,
+    w_residual_far,
     edge_ref,
     pre_ref,
     source_hot_ref,
-    w_bilinear_t_ref,
+    w_mix_ref,
     w_source_ref,
-    w_down_t_ref,
+    w_narrow_ref,
+    index_ref,
+    w_residual_ref,
+    atom_rows_ref,
     w_edge_ref,
     source_ref,
     w_bilinear_ref,
+    target_ref,
     sems,
 ):
+    f32, bf16 = jnp.float32, jnp.bfloat16
+    slots, narrow, atoms = send_far.shape[0], w_down_t_far.shape[0], atom_far.shape[0]
     copies = [
         pltpu.make_async_copy(here, there, sems.at[at])
         for at, (here, there) in enumerate(
@@ -83,19 +95,36 @@
                 (w_edge_far, w_edge_ref),
                 (source_far, source_ref),
                 (w_bilinear_far, w_bilinear_ref),
+                (target_far, target_ref),
+                (atom_far, atom_rows_ref.at[pl.ds(0, atoms), :]),
                 (w_source_far, w_source_ref),
-                (w_down_t_far, w_down_t_ref),
+                (w_down_t_far, w_narrow_ref.at[pl.ds(0, narrow), :]),
+                (w_up_far, w_narrow_ref.at[pl.ds(narrow, narrow), :]),
+                (send_far, index_ref.at[pl.ds(0, slots), :]),
+                (return_far, index_ref.at[pl.ds(slots, slots), :]),
+                (w_residual_far.at[pl.ds(0, w_residual_ref.shape[0])], w_residual_ref),
             )
         )
     ]
     for copy in copies:
         copy.start()
-    for copy in copies:
+    for copy in copies[:5]:
         copy.wait()
     pre_ref[...] = matmul(edge_ref[...], w_edge_ref[...])
-    w_bilinear_t_ref[...] = w_bilinear_ref[...].T
+    for first in range(0, w_mix_ref.shape[1], 2 * narrow):
+        w_mix_ref[:, first : first + 2 * narrow] = jnp.concatenate(
+            [
+                w_bilinear_ref[:, at : at + narrow].astype(f32).T
+                for at in (first, first + narrow)
+            ],
+            axis=1,
+        ).astype(bf16)
     hot = lax.broadcasted_iota(jnp.int32, source_hot_ref.shape[::-1], 0) == source_ref[...]
-    source_hot_ref[...] = hot.astype(jnp.float32).T.astype(jnp.bfloat16)
+    source_hot_ref[...] = hot.astype(f32).T.astype(bf16)
+    hot = lax.broadcasted_iota(jnp.int32, (atoms, target_ref.shape[1]), 0) == target_ref[...]
+    atom_rows_ref[atoms:, :] = hot.astype(f32).astype(bf16)
+    for copy in copies[5:]:
+        copy.wait()
 
 
 def main_kernel(
@@ -103,33 +132,35 @@
     edge_ref,
     pre_ref,
     source_hot_ref,
-    w_bilinear_t_ref,
+    w_mix_ref,
     w_source_ref,
-    w_down_t_ref,
-    *refs,
+    w_narrow_ref,
+    index_ref,
+    w_residual_ref,
+    atom_rows_ref,
+    w_last_far,
+    w_atom_far,
+    edge_out_ref,
+    atom_out_ref,
+    w_last_ref,
+    w_atom_ref,
+    sems,
 ):
-    count = (len(refs) - 3) // 2
-    far, (edge_out_ref, atom_out_ref) = refs[:count], refs[count : count + 2]
-    near, sems = refs[count + 2 : -1], refs[-1]
     copies = [
-        pltpu.make_async_copy(here, there, sems.at[at])
-        for at, (here, there) in enumerate(zip(far, near))
+        pltpu.make_async_copy(w_last_far.at[w_residual_ref.shape[0]], w_last_ref, sems.at[0]),
+        pltpu.make_async_copy(w_atom_far, w_atom_ref, sems.at[1]),
     ]
     for copy in copies:
         copy.start()
-    send_ref, return_ref, w_residual_ref, w_up_ref, w_atom_ref, target_ref, atom_ref = near
-
-    def ready(*ats):
-        for at in ats:
-            copies[at].wait()
-
     bf16, f32 = jnp.bfloat16, jnp.float32
     peers = recv_ref.shape[0]
-    pieces = send_ref.shape[0] // peers
+    slot_rows = index_ref.shape[0] // 2
+    pieces = slot_rows // peers
     width = pieces * LANES
     edge_count = edge_ref.shape[0]
-    proj_width = w_down_t_ref.shape[0]
-    basis_rows = w_bilinear_t_ref.shape[0] // proj_width
+    proj_width = w_mix_ref.shape[0]
+    atom_count = atom_out_ref.shape[0]
+    basis_rows = w_mix_ref.shape[1] // proj_width
     index_row = basis_rows * pieces
     atom_row = index_row + 2 * pieces
     halves = atom_out_ref.shape[1] // LANES
@@ -153,25 +184,26 @@
     activated = silu(pre_ref[...] + matmul(src_rows, w_source_ref[...])).astype(bf16)
     projected = silu(
         lax.dot_general(
-            activated, w_down_t_ref[...], (((1,), (1,)), ((), ())), preferred_element_type=f32
+            w_narrow_ref[:proj_width, :], activated, (((1,), (1,)), ((), ())), preferred_element_type=f32
         )
     ).astype(bf16)
-    expanded = lax.dot_general(
-        w_bilinear_t_ref[...], projected, (((1,), (1,)), ((), ())), preferred_element_type=f32
-    ).astype(bf16)
-
-    ready(0, 1)
+    w_mix = w_mix_ref[...]
+
     edge_iota = lax.broadcasted_iota(jnp.int32, (edge_count, LANES), 0).astype(f32).astype(bf16)
+    packed = 16
     upper = lax.broadcasted_iota(jnp.int32, (2 * pieces, LANES), 0) < pieces
     one, zero = jnp.ones((), bf16), jnp.zeros((), bf16)
 
     def one_hot(rows):
         parts = []
         for piece in range(pieces):
-            spread = jnp.broadcast_to(rows[piece : piece + 1, :], (edge_count, LANES)).astype(bf16)
+            spread = jnp.broadcast_to(rows[piece : piece + 1, :], (packed, LANES)).astype(bf16)
+            spread = jnp.concatenate([spread] * (edge_count // packed), axis=0)
             parts.append(jnp.where(spread == edge_iota, one, zero))
         return jnp.concatenate(parts, axis=1)
 
+    middle = ((edge.astype(f32) + activated.astype(f32)) * inv_root).astype(bf16)
+    inner, stage = None, 0
     total = jnp.zeros((edge_count, proj_width), f32)
     for t in range(peers):
         slots = recv_ref[t, index_row:atom_row, :].astype(f32).astype(jnp.int32) + width // 2
@@ -181,48 +213,48 @@
             here = t * pieces + r
             table = jnp.where(
                 upper,
-                jnp.broadcast_to(send_ref[here : here + 1, :], slots.shape),
-                jnp.broadcast_to(return_ref[here : here + 1, :], slots.shape),
+                jnp.broadcast_to(index_ref[here : here + 1, :], slots.shape),
+                jnp.broadcast_to(
+                    index_ref[slot_rows + here : slot_rows + here + 1, :], slots.shape
+                ),
             )
             got = jnp.take_along_axis(table, lane, axis=1, mode="promise_in_bounds")
             found = jnp.where(row == r, got, found)
         found = found.astype(f32)
         in_hot = one_hot(found[:pieces])
-        gathered = matmul(expanded, in_hot)
-        mixed = []
-        for piece in range(pieces):
-            coeffs = recv_ref[t, piece * basis_rows : (piece + 1) * basis_rows, :].astype(f32)
-            part = None
-            for k in range(basis_rows):
-                term = (
-                    gathered[k * proj_width : (k + 1) * proj_width, piece * LANES : (piece + 1) * LANES]
-                    * coeffs[k : k + 1, :]
-                )
-                part = term if part is None else part + term
-            mixed.append(part.astype(bf16))
+        rows = matmul(projected, in_hot).astype(bf16)
+        coeffs = jnp.concatenate(
+            [
+                recv_ref[t, piece * basis_rows : (piece + 1) * basis_rows, :]
+                for piece in range(pieces)
+            ],
+            axis=1,
+        )
+        terms = jnp.concatenate(
+            [rows * coeffs[k : k + 1, :] for k in range(basis_rows)], axis=0
+        )
+        mixed = matmul(w_mix, terms).astype(bf16)
         total = total + lax.dot_general(
-            one_hot(found[pieces:]),
-            jnp.concatenate(mixed, axis=1),
-            (((1,), (1,)), ((), ())),
-            preferred_element_type=f32,
-        )
-
-    ready(2, 3, 4, 5, 6)
-    base = ((edge.astype(f32) + activated.astype(f32)) * inv_root).astype(bf16)
-    inner_one = silu(matmul(base, w_residual_ref[0])).astype(bf16)
-    middle = ((base.astype(f32) + silu(matmul(inner_one, w_residual_ref[1]))) * inv_root).astype(bf16)
-    inner_two = silu(matmul(middle, w_residual_ref[2])).astype(bf16)
-    chain = (middle.astype(f32) + silu(matmul(inner_two, w_residual_ref[3]))) * inv_root
-    update = silu(matmul(total.astype(bf16), w_up_ref[...]))
+            one_hot(found[pieces:]), mixed, (((1,), (1,)), ((), ())), preferred_element_type=f32
+        )
+        if (t + 1) * w_residual_ref.shape[0] // peers > stage:
+            grown = silu(matmul(middle if stage % 2 == 0 else inner, w_residual_ref[stage]))
+            if stage % 2 == 0:
+                inner = grown.astype(bf16)
+            else:
+                middle = ((middle.astype(f32) + grown) * inv_root).astype(bf16)
+            stage += 1
+    for copy in copies:
+        copy.wait()
+    chain = (middle.astype(f32) + silu(matmul(inner, w_last_ref[...]))) * inv_root
+    update = silu(matmul(total.astype(bf16), w_narrow_ref[proj_width:, :]))
     edge_out = (chain + update).astype(bf16)
     edge_out_ref[...] = edge_out
     contrib = matmul(edge_out, w_atom_ref[...]).astype(bf16)
-    atom_count = atom_ref.shape[0]
-    target_hot = (
-        lax.broadcasted_iota(jnp.int32, (atom_count, edge_count), 0) == target_ref[...]
-    ).astype(f32).astype(bf16)
-    atom_sum = matmul(target_hot, contrib)
-    atom_out_ref[...] = (atom_ref[...].astype(f32) + silu(0.25 * atom_sum)).astype(bf16)
+    atom_sum = matmul(atom_rows_ref[atom_count:, :], contrib)
+    atom_out_ref[...] = (
+        atom_rows_ref[:atom_count, :].astype(f32) + silu(0.25 * atom_sum)
+    ).astype(bf16)
 
 
 def local_blocks(
@@ -268,43 +300,63 @@
     stay = lambda arrays: [pltpu.with_memory_space_constraint(one, pltpu.HBM) for one in arrays]
     near, far = pl.BlockSpec(memory_space=pltpu.VMEM), pl.BlockSpec(memory_space=pltpu.HBM)
     source, w_down_t = edge_source[None, :], w_down.T
+    target, send_edges, return_edges = (
+        edge_target[None, :],
+        by_lanes(send_edges),
+        by_lanes(return_edges),
+    )
+    edges, atoms = edge_state.shape[0], atom_state.shape[0]
     early = pl.pallas_call(
         ahead_kernel,
-        in_specs=[far] * 6,
-        out_specs=[near] * 6,
+        in_specs=[far] * 12,
+        out_specs=[near] * 9,
         out_shape=(
             like(edge_state),
-            jax.ShapeDtypeStruct((edge_state.shape[0], w_edge.shape[1]), jnp.float32),
-            jax.ShapeDtypeStruct((edge_state.shape[0], atom_sends.shape[0]), bf16),
-            jax.ShapeDtypeStruct(w_bilinear.shape[::-1], bf16),
+            jax.ShapeDtypeStruct((edges, w_edge.shape[1]), jnp.float32),
+            jax.ShapeDtypeStruct((edges, atom_sends.shape[0]), bf16),
+            like(w_bilinear),
             like(w_source),
-            like(w_down_t),
+            jax.ShapeDtypeStruct((2 * w_up.shape[0], w_up.shape[1]), bf16),
+            jax.ShapeDtypeStruct((2 * send_edges.shape[0], LANES), jnp.int32),
+            jax.ShapeDtypeStruct((w_residual.shape[0] - 1,) + w_residual.shape[1:], bf16),
+            jax.ShapeDtypeStruct((2 * atoms, atom_state.shape[1]), bf16),
         ),
         scratch_shapes=[
-            pltpu.VMEM(array.shape, array.dtype) for array in (w_edge, source, w_bilinear)
+            pltpu.VMEM(array.shape, array.dtype) for array in (w_edge, source, w_bilinear, target)
         ]
-        + [pltpu.SemaphoreType.DMA((6,))],
+        + [pltpu.SemaphoreType.DMA((12,))],
         compiler_params=pltpu.CompilerParams(vmem_limit_bytes=8 * 1024 * 1024),
         name="ahead",
-    )(*stay((edge_state, w_edge, source, w_bilinear, w_source, w_down_t)))
-    late = (
-        by_lanes(send_edges),
-        by_lanes(return_edges),
-        w_residual,
-        w_up,
-        w_atom,
-        edge_target[None, :],
-        atom_state,
+    )(
+        *stay(
+            (
+                edge_state,
+                w_edge,
+                source,
+                w_bilinear,
+                target,
+                atom_state,
+                w_source,
+                w_down_t,
+                send_edges,
+                return_edges,
+                w_up,
+                w_residual,
+            )
+        )
     )
     return pl.pallas_call(
         main_kernel,
-        in_specs=[near] * 7 + [far] * len(late),
+        in_specs=[near] * 10 + [far] * 2,
         out_shape=(like(edge_state), like(atom_state)),
-        scratch_shapes=[pltpu.VMEM(array.shape, array.dtype) for array in late]
-        + [pltpu.SemaphoreType.DMA((len(late),))],
+        scratch_shapes=[
+            pltpu.VMEM(w_residual.shape[1:], bf16),
+            pltpu.VMEM(w_atom.shape, bf16),
+            pltpu.SemaphoreType.DMA((2,)),
+        ],
         compiler_params=pltpu.CompilerParams(vmem_limit_bytes=32 * 1024 * 1024),
         name="block",
-    )(received, *early, *stay(late))
+    )(received, *early, *stay((w_residual, w_atom)))
 
 
 def bilinear_terms(inputs_x, coeffs, keeps, w_bilinear):

time: 32.6 us -> 30.5 us (0.936)
  Pallas kernels: 14.3 us -> 12.9 us
  waiting for transfers between devices: 10.1 us -> 9.34 us
    pallas_call x2, Pallas kernels: 12.3 us -> 10.9 us  [the longest x1 8.61 us: local_blocks(): pl.pallas_call(main_kernel, in_specs=[near] * 10 + [far] * 2, out_shape=(...]
    all_to_all x1, waiting for transfers between devices: 10.1 us -> 9.34 us  [local_blocks(): lax.all_to_all(packed, 'graph', split_axis=0, concat_axis=0, tiled=True)]
  transfers between devices with their start and end apart: 1 -> 1, of which waited for: 1 -> 1; matrix products, arithmetic and copies ran while one was open for 0% -> 0% of each run, Pallas kernels for 5% -> 8%
where the time goes in v4:
time: 30.5 us; the launch traced here: 30.2 us
  Pallas kernels  12.9 us (42%)
  waiting for transfers between devices  9.34 us (31%)
  starting transfers between devices  7.36 us (24%)
  between operations  0.65 us (2%)
    all_to_all x1, waiting for transfers between devices, local_blocks(): lax.all_to_all(packed, 'graph', split_axis=0, concat_axis=0, tiled=True)  9.34 us
    pallas_call x1, Pallas kernels, local_blocks(): pl.pallas_call(main_kernel, in_specs=[near] * 10 + [far] * 2, out_shape=(...  8.61 us
    all_to_all x1, starting transfers between devices, local_blocks(): lax.all_to_all(packed, 'graph', split_axis=0, concat_axis=0, tiled=True)  7.36 us
    pallas_call x1, Pallas kernels, local_blocks(): pl.pallas_call(ahead_kernel, in_specs=[far] * 12, out_specs=[near] * 9, o...  2.32 us
    pallas_call x1, Pallas kernels, local_blocks(): pl.pallas_call(pack_kernel, out_shape=jax.ShapeDtypeStruct((peers, rows,...  1.93 us
  transfers between devices with their start and end apart: 1, of which 1 were waited for; matrix products, arithmetic and copies ran while one was open for 0% of the time, Pallas kernels for 8%

profile of v4, /device:TPU:0, one launch (start us, length us, event | category | flops | bytes accessed | tf_op | source)
XLA Modules:
  0.0 30.2 jit_solution(14878124526013275114)
XLA Ops:
  0.6 1.9 %pack.1 = bf16[16,88,128]{2,1,0:T(8,128)(2,1)} custom-call(bf16[16,8192]{1,0:T(8,128)(2,1)} %basis_ref.1, s32[64,128]{1,0:T(8,128)} %bitcast.12, s32[64,128]{1,0:T(8,128)} %bitcast.13, s32[64,128]{1,0:T(8,128)} %bitcast.14, bf16[16,256]{1,0:T(8,128)(2,1)} %atom_far.1, s32[1,128]{1,0:T(1,128)} %bitcast.17), custom_call_target="tpu_custom_call" | custom-call | tf_op jit(solution)/shard_map/pack/pallas_call | solution.py:286
  2.6 7.4 %all-to-all-start = ((bf16[16,88,128]{2,1,0:T(8,128)(2,1)}), bf16[16,88,128]{2,1,0:T(8,128)(2,1)S(1)}, u32[]{:S(2)}, u32[]{:S(2)}) async-start(bf16[16,88,128]{2,1,0:T(8,128)(2,1)} %pack.1), calls=%async_computation | async-start | bytes 720896 | tf_op jit(solution)/shard_map/all_to_all | solution.py:298
  9.9 2.3 %ahead.1 = (bf16[256,512]{1,0:T(8,128)(2,1)S(1)}, f32[256,512]{1,0:T(8,128)S(1)}, bf16[256,128]{1,0:T(8,128)(2,1)S(1)}, bf16[64,1024]{1,0:T(8,128)(2,1)S(1)}, bf...) custom-call(bf16[256,512]{1,0:T(8,128)(2,1)} %edge_far.1, ...), custom_call_target="tpu_custom_call" | custom-call | tf_op jit(solution)/shard_map/ahead/pallas_call | solution.py:309
  12.3 9.3 %all-to-all-done.recv_ref = bf16[16,88,128]{2,1,0:T(8,128)(2,1)S(1)} async-done(((bf16[16,88,128]{2,1,0:T(8,128)(2,1)}), bf16[16,88,128]{2,1,0:T(8,128)(2,1)S(1)}, u32[]{:S(2)}, u32[]{:S(2)}) %all-to-all-start) | async-done | bytes 360480 | tf_op jit(solution)/shard_map/all_to_all | solution.py:298
  21.6 8.6 %block.1 = (bf16[256,512]{1,0:T(8,128)(2,1)}, bf16[16,256]{1,0:T(8,128)(2,1)}) custom-call(bf16[16,88,128]{2,1,0:T(8,128)(2,1)S(1)} %all-to-all-done.recv_ref, bf16[256,512]{1,0:T(8,128)(2,1)S(1)} %get-tuple-element.11.edge_ref, f32[256,512]{1,0:T(8,128)S(1)} %get-tuple-element.12.pre_ref, bf16[256,128]{1,0:T(8,128)(2,1)S(1)} %get-tuple-element.13.source_hot_ref, ...), custom_call_target="tpu_custom_call" | custom-call | tf_op jit(solution)/shard_map/block/pallas_call | solution.py:348
Async XLA Ops:
  2.6 19.0 %all-to-all-start = ((bf16[16,88,128]{2,1,0:T(8,128)(2,1)}), bf16[16,88,128]{2,1,0:T(8,128)(2,1)S(1)}, u32[]{:S(2)}, u32[]{:S(2)}) async-start(bf16[16,88,128]{2,1,0:T(8,128)(2,1)} %pack.1), calls=%async_computation | async-start | bytes 720896 | tf_op jit(solution)/shard_map/all_to_all | solution.py:298

commit v5 on v4

--- a/solution.py
+++ b/solution.py
@@ -7,6 +7,7 @@
 
 WIN = 512
 LANES = 128
+GROWN = 6
 
 
 inv_root = 0.7071067811865476
@@ -74,6 +75,7 @@
     pre_ref,
     source_hot_ref,
     w_mix_ref,
+    w_grow_ref,
     w_source_ref,
     w_narrow_ref,
     index_ref,
@@ -111,14 +113,17 @@
     for copy in copies[:5]:
         copy.wait()
     pre_ref[...] = matmul(edge_ref[...], w_edge_ref[...])
-    for first in range(0, w_mix_ref.shape[1], 2 * narrow):
-        w_mix_ref[:, first : first + 2 * narrow] = jnp.concatenate(
-            [
-                w_bilinear_ref[:, at : at + narrow].astype(f32).T
-                for at in (first, first + narrow)
-            ],
-            axis=1,
-        ).astype(bf16)
+    grown = w_grow_ref.shape[0]
+    for first in range(0, w_bilinear_ref.shape[1], 2 * narrow):
+        pair = [
+            w_bilinear_ref[:, at : at + narrow].astype(f32).T for at in (first, first + narrow)
+        ]
+        if first < grown:
+            w_grow_ref[first : first + 2 * narrow, :] = jnp.concatenate(pair, axis=0).astype(bf16)
+        else:
+            w_mix_ref[:, first - grown : first - grown + 2 * narrow] = jnp.concatenate(
+                pair, axis=1
+            ).astype(bf16)
     hot = lax.broadcasted_iota(jnp.int32, source_hot_ref.shape[::-1], 0) == source_ref[...]
     source_hot_ref[...] = hot.astype(f32).T.astype(bf16)
     hot = lax.broadcasted_iota(jnp.int32, (atoms, target_ref.shape[1]), 0) == target_ref[...]
@@ -133,6 +138,7 @@
     pre_ref,
     source_hot_ref,
     w_mix_ref,
+    w_grow_ref,
     w_source_ref,
     w_narrow_ref,
     index_ref,
@@ -160,7 +166,8 @@
     edge_count = edge_ref.shape[0]
     proj_width = w_mix_ref.shape[0]
     atom_count = atom_out_ref.shape[0]
-    basis_rows = w_mix_ref.shape[1] // proj_width
+    grown = w_grow_ref.shape[0] // proj_width
+    basis_rows = w_mix_ref.shape[1] // proj_width + grown
     index_row = basis_rows * pieces
     atom_row = index_row + 2 * pieces
     halves = atom_out_ref.shape[1] // LANES
@@ -188,6 +195,9 @@
         )
     ).astype(bf16)
     w_mix = w_mix_ref[...]
+    table = jnp.concatenate(
+        [projected, matmul(w_grow_ref[...], projected).astype(bf16)], axis=0
+    )
 
     edge_iota = lax.broadcasted_iota(jnp.int32, (edge_count, LANES), 0).astype(f32).astype(bf16)
     packed = 16
@@ -204,45 +214,69 @@
 
     middle = ((edge.astype(f32) + activated.astype(f32)) * inv_root).astype(bf16)
     inner, stage = None, 0
-    total = jnp.zeros((edge_count, proj_width), f32)
-    for t in range(peers):
+
+    def basis_of(t):
+        return jnp.concatenate(
+            [
+                recv_ref[t, piece * basis_rows : (piece + 1) * basis_rows, :]
+                for piece in range(pieces)
+            ],
+            axis=1,
+        )
+
+    def choose(t):
         slots = recv_ref[t, index_row:atom_row, :].astype(f32).astype(jnp.int32) + width // 2
         lane, row = slots % LANES, slots // LANES
         found = jnp.zeros(slots.shape, jnp.int32)
         for r in range(pieces):
             here = t * pieces + r
-            table = jnp.where(
+            places = jnp.where(
                 upper,
                 jnp.broadcast_to(index_ref[here : here + 1, :], slots.shape),
                 jnp.broadcast_to(
                     index_ref[slot_rows + here : slot_rows + here + 1, :], slots.shape
                 ),
             )
-            got = jnp.take_along_axis(table, lane, axis=1, mode="promise_in_bounds")
+            got = jnp.take_along_axis(places, lane, axis=1, mode="promise_in_bounds")
             found = jnp.where(row == r, got, found)
         found = found.astype(f32)
-        in_hot = one_hot(found[:pieces])
-        rows = matmul(projected, in_hot).astype(bf16)
-        coeffs = jnp.concatenate(
-            [
-                recv_ref[t, piece * basis_rows : (piece + 1) * basis_rows, :]
-                for piece in range(pieces)
-            ],
-            axis=1,
-        )
+        rows = matmul(table, one_hot(found[:pieces]))
+        near = None
+        coeffs = basis_of(t)
+        for k in range(grown):
+            term = rows[(k + 1) * proj_width : (k + 2) * proj_width, :] * coeffs[
+                k : k + 1, :
+            ].astype(f32)
+            near = term if near is None else near + term
+        return rows[:proj_width].astype(bf16), found[pieces:], near
+
+    def mix(t, rows, near):
+        coeffs = basis_of(t)
         terms = jnp.concatenate(
-            [rows * coeffs[k : k + 1, :] for k in range(basis_rows)], axis=0
-        )
-        mixed = matmul(w_mix, terms).astype(bf16)
-        total = total + lax.dot_general(
-            one_hot(found[pieces:]), mixed, (((1,), (1,)), ((), ())), preferred_element_type=f32
-        )
-        if (t + 1) * w_residual_ref.shape[0] // peers > stage:
-            grown = silu(matmul(middle if stage % 2 == 0 else inner, w_residual_ref[stage]))
+            [rows * coeffs[k : k + 1, :] for k in range(grown, basis_rows)], axis=0
+        )
+        return (matmul(w_mix, terms) + near).astype(bf16)
+
+    def spread(mixed, targets):
+        return lax.dot_general(
+            one_hot(targets), mixed, (((1,), (1,)), ((), ())), preferred_element_type=f32
+        )
+
+    total = jnp.zeros((edge_count, proj_width), f32)
+    chosen, mixes = {}, {}
+    for step in range(peers + 2):
+        if step < peers:
+            chosen[step] = choose(step)
+        if 0 <= step - 1 < peers:
+            mixes[step - 1] = mix(step - 1, chosen[step - 1][0], chosen[step - 1][2])
+        if 0 <= step - 2 < peers:
+            total = total + spread(mixes.pop(step - 2), chosen.pop(step - 2)[1])
+        if step < peers and (step + 1) * w_residual_ref.shape[0] // peers > stage:
+            fresh = silu(matmul(middle if stage % 2 == 0 else inner, w_residual_ref[stage]))
             if stage % 2 == 0:
-                inner = grown.astype(bf16)
+                inner = fresh.astype(bf16)
             else:
-                middle = ((middle.astype(f32) + grown) * inv_root).astype(bf16)
+                middle = ((middle.astype(f32) + fresh) * inv_root).astype(bf16)
             stage += 1
     for copy in copies:
         copy.wait()
@@ -306,15 +340,18 @@
         by_lanes(return_edges),
     )
     edges, atoms = edge_state.shape[0], atom_state.shape[0]
+    narrow = w_up.shape[0]
+    grown = GROWN * narrow
     early = pl.pallas_call(
         ahead_kernel,
         in_specs=[far] * 12,
-        out_specs=[near] * 9,
+        out_specs=[near] * 10,
         out_shape=(
             like(edge_state),
             jax.ShapeDtypeStruct((edges, w_edge.shape[1]), jnp.float32),
             jax.ShapeDtypeStruct((edges, atom_sends.shape[0]), bf16),
-            like(w_bilinear),
+            jax.ShapeDtypeStruct((narrow, w_bilinear.shape[1] - grown), bf16),
+            jax.ShapeDtypeStruct((grown, narrow), bf16),
             like(w_source),
             jax.ShapeDtypeStruct((2 * w_up.shape[0], w_up.shape[1]), bf16),
             jax.ShapeDtypeStruct((2 * send_edges.shape[0], LANES), jnp.int32),
@@ -347,7 +384,7 @@
     )
     return pl.pallas_call(
         main_kernel,
-        in_specs=[near] * 10 + [far] * 2,
+        in_specs=[near] * 11 + [far] * 2,
         out_shape=(like(edge_state), like(atom_state)),
         scratch_shapes=[
             pltpu.VMEM(w_residual.shape[1:], bf16),

time: 30.5 us -> 29.2 us (0.957)
  Pallas kernels: 12.9 us -> 11.3 us
  waiting for transfers between devices: 9.34 us -> 9.66 us
    pallas_call x2, Pallas kernels: 10.9 us -> 9.33 us  [the longest x1 7.32 us: local_blocks(): pl.pallas_call(main_kernel, in_specs=[near] * 11 + [far] * 2, out_shape=(...]
    all_to_all x1, waiting for transfers between devices: 9.34 us -> 9.66 us  [local_blocks(): lax.all_to_all(packed, 'graph', split_axis=0, concat_axis=0, tiled=True)]
  transfers between devices with their start and end apart: 1 -> 1, of which waited for: 1 -> 1; matrix products, arithmetic and copies ran while one was open for 0% -> 0% of each run, Pallas kernels for 8% -> 7%
where the time goes in v5:
time: 29.2 us; the launch traced here: 28.9 us
  Pallas kernels  11.3 us (39%)
  waiting for transfers between devices  9.66 us (33%)
  starting transfers between devices  7.36 us (25%)
  between operations  0.65 us (2%)
    all_to_all x1, waiting for transfers between devices, local_blocks(): lax.all_to_all(packed, 'graph', split_axis=0, concat_axis=0, tiled=True)  9.66 us
    all_to_all x1, starting transfers between devices, local_blocks(): lax.all_to_all(packed, 'graph', split_axis=0, concat_axis=0, tiled=True)  7.36 us
    pallas_call x1, Pallas kernels, local_blocks(): pl.pallas_call(main_kernel, in_specs=[near] * 11 + [far] * 2, out_shape=(...  7.32 us
    pallas_call x1, Pallas kernels, local_blocks(): pl.pallas_call(ahead_kernel, in_specs=[far] * 12, out_specs=[near] * 10,...  2.01 us
    pallas_call x1, Pallas kernels, local_blocks(): pl.pallas_call(pack_kernel, out_shape=jax.ShapeDtypeStruct((peers, rows,...  1.93 us
  transfers between devices with their start and end apart: 1, of which 1 were waited for; matrix products, arithmetic and copies ran while one was open for 0% of the time, Pallas kernels for 7%

profile of v5, /device:TPU:0, one launch (start us, length us, event | category | flops | bytes accessed | tf_op | source)
XLA Modules:
  0.0 28.9 jit_solution(4322043720680598535)
XLA Ops:
  0.6 1.9 %pack.1 = bf16[16,88,128]{2,1,0:T(8,128)(2,1)} custom-call(bf16[16,8192]{1,0:T(8,128)(2,1)} %basis_ref.1, s32[64,128]{1,0:T(8,128)} %bitcast.12, s32[64,128]{1,0:T(8,128)} %bitcast.13, s32[64,128]{1,0:T(8,128)} %bitcast.14, bf16[16,256]{1,0:T(8,128)(2,1)} %atom_far.1, s32[1,128]{1,0:T(1,128)} %bitcast.17), custom_call_target="tpu_custom_call" | custom-call | tf_op jit(solution)/shard_map/pack/pallas_call | solution.py:320
  2.6 7.4 %all-to-all-start = ((bf16[16,88,128]{2,1,0:T(8,128)(2,1)}), bf16[16,88,128]{2,1,0:T(8,128)(2,1)S(1)}, u32[]{:S(2)}, u32[]{:S(2)}) async-start(bf16[16,88,128]{2,1,0:T(8,128)(2,1)} %pack.1), calls=%async_computation | async-start | bytes 720896 | tf_op jit(solution)/shard_map/all_to_all | solution.py:332
  9.9 2.0 %ahead.1 = (bf16[256,512]{1,0:T(8,128)(2,1)S(1)}, f32[256,512]{1,0:T(8,128)S(1)}, bf16[256,128]{1,0:T(8,128)(2,1)S(1)}, bf16[64,640]{1,0:T(8,128)(2,1)S(1)}, bf1...) custom-call(bf16[256,512]{1,0:T(8,128)(2,1)} %edge_far.1, ...), custom_call_target="tpu_custom_call" | custom-call | tf_op jit(solution)/shard_map/ahead/pallas_call | solution.py:345
  11.9 9.7 %all-to-all-done.recv_ref = bf16[16,88,128]{2,1,0:T(8,128)(2,1)S(1)} async-done(((bf16[16,88,128]{2,1,0:T(8,128)(2,1)}), bf16[16,88,128]{2,1,0:T(8,128)(2,1)S(1)}, u32[]{:S(2)}, u32[]{:S(2)}) %all-to-all-start) | async-done | bytes 360480 | tf_op jit(solution)/shard_map/all_to_all | solution.py:332
  21.6 7.3 %block.1 = (bf16[256,512]{1,0:T(8,128)(2,1)}, bf16[16,256]{1,0:T(8,128)(2,1)}) custom-call(bf16[16,88,128]{2,1,0:T(8,128)(2,1)S(1)} %all-to-all-done.recv_ref, bf16[256,512]{1,0:T(8,128)(2,1)S(1)} %get-tuple-element.12.edge_ref, f32[256,512]{1,0:T(8,128)S(1)} %get-tuple-element.13.pre_ref, bf16[256,128]{1,0:T(8,128)(2,1)S(1)} %get-tuple-element.14.source_hot_ref, ...), custom_call_target="tpu_custom_call" | custom-call | tf_op jit(solution)/shard_map/block/pallas_call | solution.py:385
Async XLA Ops:
  2.6 19.0 %all-to-all-start = ((bf16[16,88,128]{2,1,0:T(8,128)(2,1)}), bf16[16,88,128]{2,1,0:T(8,128)(2,1)S(1)}, u32[]{:S(2)}, u32[]{:S(2)}) async-start(bf16[16,88,128]{2,1,0:T(8,128)(2,1)} %pack.1), calls=%async_computation | async-start | bytes 720896 | tf_op jit(solution)/shard_map/all_to_all | solution.py:332

commit v6 on v5

--- a/solution.py
+++ b/solution.py
@@ -28,9 +28,49 @@
     return (0.5 * v) * (1.0 + jnp.tanh(0.5 * v))
 
 
-def pack_kernel(basis_ref, valid_ref, in_ref, out_ref, atom_ref, sends_ref, send_ref):
-    basis_rows = basis_ref.shape[0]
-    peers = send_ref.shape[0]
+def pack_kernel(
+    basis_far,
+    valid_far,
+    in_far,
+    out_far,
+    atom_far,
+    sends_far,
+    send_far,
+    basis_ref,
+    valid_ref,
+    in_ref,
+    out_ref,
+    atom_ref,
+    sends_ref,
+    send_ref,
+    sems,
+    done_sems,
+):
+    peers, parts = send_ref.shape[0], done_sems.shape[0]
+    span, columns = peers // parts, basis_ref.shape[1] // parts
+    copies = [
+        pltpu.make_async_copy(here, there, sems.at[at])
+        for at, (here, there) in enumerate(
+            [
+                (atom_far, atom_ref),
+                (sends_far, sends_ref),
+                (valid_far, valid_ref),
+                (in_far, in_ref),
+                (out_far, out_ref),
+            ]
+            + [
+                (
+                    basis_far.at[:, pl.ds(part * columns, columns)],
+                    basis_ref.at[:, pl.ds(part * columns, columns)],
+                )
+                for part in range(parts)
+            ]
+        )
+    ]
+    for copy in copies:
+        copy.start()
+    for copy in copies[:5]:
+        copy.wait()
     pieces = valid_ref.shape[0] // peers
     width = pieces * LANES
     atom_slots = sends_ref.shape[1]
@@ -41,21 +81,33 @@
     rows = lax.dot_general(
         chooser, atom_ref[...], (((0,), (0,)), ((), ())), preferred_element_type=jnp.float32
     ).astype(jnp.bfloat16)
-    keeps = valid_ref[...].astype(jnp.float32)
+    keeps = valid_ref[...].astype(jnp.float32).astype(jnp.bfloat16)
     half = width // 2
     local_in = ((in_ref[...] % width) - half).astype(jnp.float32).astype(jnp.bfloat16)
     local_out = ((out_ref[...] % width) - half).astype(jnp.float32).astype(jnp.bfloat16)
-    for peer in range(peers):
-        parts = []
-        for piece in range(pieces):
-            row = peer * pieces + piece
-            tile = basis_ref[:, row * LANES : (row + 1) * LANES].astype(jnp.float32)
-            parts.append((tile * keeps[row : row + 1, :]).astype(jnp.bfloat16))
-        parts.append(local_in[peer * pieces : (peer + 1) * pieces, :])
-        parts.append(local_out[peer * pieces : (peer + 1) * pieces, :])
-        for first in range(0, atom_ref.shape[1], LANES):
-            parts.append(rows[peer * cap_a : (peer + 1) * cap_a, first : first + LANES])
-        send_ref[peer] = jnp.concatenate(parts, axis=0)
+    sent = []
+    for part in range(parts):
+        copies[5 + part].wait()
+        for peer in range(part * span, (part + 1) * span):
+            blocks = []
+            for piece in range(pieces):
+                row = peer * pieces + piece
+                blocks.append(basis_ref[:, row * LANES : (row + 1) * LANES] * keeps[row : row + 1, :])
+            blocks.append(local_in[peer * pieces : (peer + 1) * pieces, :])
+            blocks.append(local_out[peer * pieces : (peer + 1) * pieces, :])
+            for first in range(0, atom_ref.shape[1], LANES):
+                blocks.append(rows[peer * cap_a : (peer + 1) * cap_a, first : first + LANES])
+            send_ref[peer] = jnp.concatenate(blocks, axis=0)
+        sent.append(
+            pltpu.make_async_copy(
+                send_ref.at[pl.ds(part * span, span)],
+                send_far.at[pl.ds(part * span, span)],
+                done_sems.at[part],
+            )
+        )
+        sent[-1].start()
+    for copy in sent:
+        copy.wait()
 
 
 def ahead_kernel(
@@ -248,7 +300,7 @@
                 k : k + 1, :
             ].astype(f32)
             near = term if near is None else near + term
-        return rows[:proj_width].astype(bf16), found[pieces:], near
+        return rows[:proj_width].astype(bf16), one_hot(found[pieces:]), near
 
     def mix(t, rows, near):
         coeffs = basis_of(t)
@@ -259,7 +311,7 @@
 
     def spread(mixed, targets):
         return lax.dot_general(
-            one_hot(targets), mixed, (((1,), (1,)), ((), ())), preferred_element_type=f32
+            targets, mixed, (((1,), (1,)), ((), ())), preferred_element_type=f32
         )
 
     total = jnp.zeros((edge_count, proj_width), f32)
@@ -317,11 +369,10 @@
     rows = triplet_basis.shape[0] * pieces + 2 * pieces
     rows += atom_sends.shape[0] // peers * (atom_state.shape[1] // LANES)
     by_lanes = lambda array: array.reshape(-1, LANES)
-    packed = pl.pallas_call(
-        pack_kernel,
-        out_shape=jax.ShapeDtypeStruct((peers, rows, LANES), bf16),
-        name="pack",
-    )(
+    like = lambda array: jax.ShapeDtypeStruct(array.shape, array.dtype)
+    stay = lambda arrays: [pltpu.with_memory_space_constraint(one, pltpu.HBM) for one in arrays]
+    near, far = pl.BlockSpec(memory_space=pltpu.VMEM), pl.BlockSpec(memory_space=pltpu.HBM)
+    inputs = (
         triplet_basis,
         by_lanes(triplet_valid),
         by_lanes(triplet_in),
@@ -329,10 +380,21 @@
         atom_state,
         atom_sends[None, :],
     )
+    parts = 4 if peers % 4 == 0 else 1
+    packed = pl.pallas_call(
+        pack_kernel,
+        in_specs=[far] * len(inputs),
+        out_specs=far,
+        out_shape=jax.ShapeDtypeStruct((peers, rows, LANES), bf16),
+        scratch_shapes=[pltpu.VMEM(one.shape, one.dtype) for one in inputs]
+        + [
+            pltpu.VMEM((peers, rows, LANES), bf16),
+            pltpu.SemaphoreType.DMA((len(inputs) - 1 + parts,)),
+            pltpu.SemaphoreType.DMA((parts,)),
+        ],
+        name="pack",
+    )(*stay(inputs))
     received = lax.all_to_all(packed, "graph", split_axis=0, concat_axis=0, tiled=True)
-    like = lambda array: jax.ShapeDtypeStruct(array.shape, array.dtype)
-    stay = lambda arrays: [pltpu.with_memory_space_constraint(one, pltpu.HBM) for one in arrays]
-    near, far = pl.BlockSpec(memory_space=pltpu.VMEM), pl.BlockSpec(memory_space=pltpu.HBM)
     source, w_down_t = edge_source[None, :], w_down.T
     target, send_edges, return_edges = (
         edge_target[None, :],

time: 29.2 us -> 29.2 us (level)
  no operation moved by 1% of the time
where the time goes in v6:
time: 29.2 us; the launch traced here: 28.9 us
  Pallas kernels  11.3 us (39%)
  waiting for transfers between devices  9.66 us (33%)
  starting transfers between devices  7.37 us (25%)
  between operations  0.66 us (2%)
    all_to_all x1, waiting for transfers between devices, local_blocks(): lax.all_to_all(packed, 'graph', split_axis=0, concat_axis=0, tiled=True)  9.66 us
    all_to_all x1, starting transfers between devices, local_blocks(): lax.all_to_all(packed, 'graph', split_axis=0, concat_axis=0, tiled=True)  7.37 us
    pallas_call x1, Pallas kernels, local_blocks(): pl.pallas_call(main_kernel, in_specs=[near] * 11 + [far] * 2, out_shape=(...  7.33 us
    pallas_call x1, Pallas kernels, local_blocks(): pl.pallas_call(ahead_kernel, in_specs=[far] * 12, out_specs=[near] * 10,...  2.01 us
    pallas_call x1, Pallas kernels, local_blocks(): pl.pallas_call(pack_kernel, in_specs=[far] * len(inputs), out_specs=far,...  1.91 us
  transfers between devices with their start and end apart: 1, of which 1 were waited for; matrix products, arithmetic and copies ran while one was open for 0% of the time, Pallas kernels for 7%

profile of v6, /device:TPU:0, one launch (start us, length us, event | category | flops | bytes accessed | tf_op | source)
XLA Modules:
  0.0 28.9 jit_solution(9005953631199918804)
XLA Ops:
  0.6 1.9 %pack.1 = bf16[16,88,128]{2,1,0:T(8,128)(2,1)} custom-call(bf16[16,8192]{1,0:T(8,128)(2,1)} %basis_far.1, s32[64,128]{1,0:T(8,128)} %bitcast.12, s32[64,128]{1,0:T(8,128)} %bitcast.13, s32[64,128]{1,0:T(8,128)} %bitcast.14, bf16[16,256]{1,0:T(8,128)(2,1)} %atom_far.3, s32[1,128]{1,0:T(1,128)} %bitcast.17), custom_call_target="tpu_custom_call" | custom-call | tf_op jit(solution)/shard_map/pack/pallas_call | solution.py:384
  2.6 7.4 %all-to-all-start = ((bf16[16,88,128]{2,1,0:T(8,128)(2,1)}), bf16[16,88,128]{2,1,0:T(8,128)(2,1)S(1)}, u32[]{:S(2)}, u32[]{:S(2)}) async-start(bf16[16,88,128]{2,1,0:T(8,128)(2,1)} %pack.1), calls=%async_computation | async-start | bytes 720896 | tf_op jit(solution)/shard_map/all_to_all | solution.py:397
  9.9 2.0 %ahead.1 = (bf16[256,512]{1,0:T(8,128)(2,1)S(1)}, f32[256,512]{1,0:T(8,128)S(1)}, bf16[256,128]{1,0:T(8,128)(2,1)S(1)}, bf16[64,640]{1,0:T(8,128)(2,1)S(1)}, bf1...) custom-call(bf16[256,512]{1,0:T(8,128)(2,1)} %edge_far.1, ...), custom_call_target="tpu_custom_call" | custom-call | tf_op jit(solution)/shard_map/ahead/pallas_call | solution.py:407
  11.9 9.7 %all-to-all-done.recv_ref = bf16[16,88,128]{2,1,0:T(8,128)(2,1)S(1)} async-done(((bf16[16,88,128]{2,1,0:T(8,128)(2,1)}), bf16[16,88,128]{2,1,0:T(8,128)(2,1)S(1)}, u32[]{:S(2)}, u32[]{:S(2)}) %all-to-all-start) | async-done | bytes 360480 | tf_op jit(solution)/shard_map/all_to_all | solution.py:397
  21.6 7.3 %block.1 = (bf16[256,512]{1,0:T(8,128)(2,1)}, bf16[16,256]{1,0:T(8,128)(2,1)}) custom-call(bf16[16,88,128]{2,1,0:T(8,128)(2,1)S(1)} %all-to-all-done.recv_ref, bf16[256,512]{1,0:T(8,128)(2,1)S(1)} %get-tuple-element.12.edge_ref, f32[256,512]{1,0:T(8,128)S(1)} %get-tuple-element.13.pre_ref, bf16[256,128]{1,0:T(8,128)(2,1)S(1)} %get-tuple-element.14.source_hot_ref, ...), custom_call_target="tpu_custom_call" | custom-call | tf_op jit(solution)/shard_map/block/pallas_call | solution.py:447
Async XLA Ops:
  2.6 19.0 %all-to-all-start = ((bf16[16,88,128]{2,1,0:T(8,128)(2,1)}), bf16[16,88,128]{2,1,0:T(8,128)(2,1)S(1)}, u32[]{:S(2)}, u32[]{:S(2)}) async-start(bf16[16,88,128]{2,1,0:T(8,128)(2,1)} %pack.1), calls=%async_computation | async-start | bytes 720896 | tf_op jit(solution)/shard_map/all_to_all | solution.py:397

commit v7 on v5

--- a/solution.py
+++ b/solution.py
@@ -248,7 +248,7 @@
                 k : k + 1, :
             ].astype(f32)
             near = term if near is None else near + term
-        return rows[:proj_width].astype(bf16), found[pieces:], near
+        return rows[:proj_width].astype(bf16), one_hot(found[pieces:]), near
 
     def mix(t, rows, near):
         coeffs = basis_of(t)
@@ -259,7 +259,7 @@
 
     def spread(mixed, targets):
         return lax.dot_general(
-            one_hot(targets), mixed, (((1,), (1,)), ((), ())), preferred_element_type=f32
+            targets, mixed, (((1,), (1,)), ((), ())), preferred_element_type=f32
         )
 
     total = jnp.zeros((edge_count, proj_width), f32)

time: 29.2 us -> 29.2 us (level)
  no operation moved by 1% of the time
where the time goes in v7:
time: 29.2 us; the launch traced here: 28.9 us
  Pallas kernels  11.3 us (39%)
  waiting for transfers between devices  9.66 us (33%)
  starting transfers between devices  7.36 us (25%)
  between operations  0.65 us (2%)
    all_to_all x1, waiting for transfers between devices, local_blocks(): lax.all_to_all(packed, 'graph', split_axis=0, concat_axis=0, tiled=True)  9.66 us
    all_to_all x1, starting transfers between devices, local_blocks(): lax.all_to_all(packed, 'graph', split_axis=0, concat_axis=0, tiled=True)  7.36 us
    pallas_call x1, Pallas kernels, local_blocks(): pl.pallas_call(main_kernel, in_specs=[near] * 11 + [far] * 2, out_shape=(...  7.32 us
    pallas_call x1, Pallas kernels, local_blocks(): pl.pallas_call(ahead_kernel, in_specs=[far] * 12, out_specs=[near] * 10,...  2.01 us
    pallas_call x1, Pallas kernels, local_blocks(): pl.pallas_call(pack_kernel, out_shape=jax.ShapeDtypeStruct((peers, rows,...  1.93 us
  transfers between devices with their start and end apart: 1, of which 1 were waited for; matrix products, arithmetic and copies ran while one was open for 0% of the time, Pallas kernels for 7%

profile of v7, /device:TPU:0, one launch (start us, length us, event | category | flops | bytes accessed | tf_op | source)
XLA Modules:
  0.0 28.9 jit_solution(4322043720680598535)
XLA Ops:
  0.6 1.9 %pack.1 = bf16[16,88,128]{2,1,0:T(8,128)(2,1)} custom-call(bf16[16,8192]{1,0:T(8,128)(2,1)} %basis_ref.1, s32[64,128]{1,0:T(8,128)} %bitcast.12, s32[64,128]{1,0:T(8,128)} %bitcast.13, s32[64,128]{1,0:T(8,128)} %bitcast.14, bf16[16,256]{1,0:T(8,128)(2,1)} %atom_far.1, s32[1,128]{1,0:T(1,128)} %bitcast.17), custom_call_target="tpu_custom_call" | custom-call | tf_op jit(solution)/shard_map/pack/pallas_call | solution.py:320
  2.6 7.4 %all-to-all-start = ((bf16[16,88,128]{2,1,0:T(8,128)(2,1)}), bf16[16,88,128]{2,1,0:T(8,128)(2,1)S(1)}, u32[]{:S(2)}, u32[]{:S(2)}) async-start(bf16[16,88,128]{2,1,0:T(8,128)(2,1)} %pack.1), calls=%async_computation | async-start | bytes 720896 | tf_op jit(solution)/shard_map/all_to_all | solution.py:332
  9.9 2.0 %ahead.1 = (bf16[256,512]{1,0:T(8,128)(2,1)S(1)}, f32[256,512]{1,0:T(8,128)S(1)}, bf16[256,128]{1,0:T(8,128)(2,1)S(1)}, bf16[64,640]{1,0:T(8,128)(2,1)S(1)}, bf1...) custom-call(bf16[256,512]{1,0:T(8,128)(2,1)} %edge_far.1, ...), custom_call_target="tpu_custom_call" | custom-call | tf_op jit(solution)/shard_map/ahead/pallas_call | solution.py:345
  11.9 9.7 %all-to-all-done.recv_ref = bf16[16,88,128]{2,1,0:T(8,128)(2,1)S(1)} async-done(((bf16[16,88,128]{2,1,0:T(8,128)(2,1)}), bf16[16,88,128]{2,1,0:T(8,128)(2,1)S(1)}, u32[]{:S(2)}, u32[]{:S(2)}) %all-to-all-start) | async-done | bytes 360480 | tf_op jit(solution)/shard_map/all_to_all | solution.py:332
  21.6 7.3 %block.1 = (bf16[256,512]{1,0:T(8,128)(2,1)}, bf16[16,256]{1,0:T(8,128)(2,1)}) custom-call(bf16[16,88,128]{2,1,0:T(8,128)(2,1)S(1)} %all-to-all-done.recv_ref, bf16[256,512]{1,0:T(8,128)(2,1)S(1)} %get-tuple-element.12.edge_ref, f32[256,512]{1,0:T(8,128)S(1)} %get-tuple-element.13.pre_ref, bf16[256,128]{1,0:T(8,128)(2,1)S(1)} %get-tuple-element.14.source_hot_ref, ...), custom_call_target="tpu_custom_call" | custom-call | tf_op jit(solution)/shard_map/block/pallas_call | solution.py:385
Async XLA Ops:
  2.6 19.0 %all-to-all-start = ((bf16[16,88,128]{2,1,0:T(8,128)(2,1)}), bf16[16,88,128]{2,1,0:T(8,128)(2,1)S(1)}, u32[]{:S(2)}, u32[]{:S(2)}) async-start(bf16[16,88,128]{2,1,0:T(8,128)(2,1)} %pack.1), calls=%async_computation | async-start | bytes 720896 | tf_op jit(solution)/shard_map/all_to_all | solution.py:332

commit v8 on v7

--- a/solution.py
+++ b/solution.py
@@ -240,7 +240,10 @@
             got = jnp.take_along_axis(places, lane, axis=1, mode="promise_in_bounds")
             found = jnp.where(row == r, got, found)
         found = found.astype(f32)
-        rows = matmul(table, one_hot(found[:pieces]))
+        return one_hot(found[:pieces]), one_hot(found[pieces:])
+
+    def gather(t, hot, targets):
+        rows = matmul(table, hot)
         near = None
         coeffs = basis_of(t)
         for k in range(grown):
@@ -248,7 +251,7 @@
                 k : k + 1, :
             ].astype(f32)
             near = term if near is None else near + term
-        return rows[:proj_width].astype(bf16), one_hot(found[pieces:]), near
+        return rows[:proj_width].astype(bf16), targets, near
 
     def mix(t, rows, near):
         coeffs = basis_of(t)
@@ -263,10 +266,14 @@
         )
 
     total = jnp.zeros((edge_count, proj_width), f32)
-    chosen, mixes = {}, {}
+    chosen, mixes, hots = {}, {}, {}
     for step in range(peers + 2):
+        if step == 0:
+            hots[0] = choose(0)
+        if step + 1 < peers:
+            hots[step + 1] = choose(step + 1)
         if step < peers:
-            chosen[step] = choose(step)
+            chosen[step] = gather(step, *hots.pop(step))
         if 0 <= step - 1 < peers:
             mixes[step - 1] = mix(step - 1, chosen[step - 1][0], chosen[step - 1][2])
         if 0 <= step - 2 < peers:

time: 29.2 us -> 29.2 us (level)
  no operation moved by 1% of the time
where the time goes in v8:
time: 29.2 us; the launch traced here: 28.9 us
  Pallas kernels  11.3 us (39%)
  waiting for transfers between devices  9.66 us (33%)
  starting transfers between devices  7.36 us (25%)
  between operations  0.65 us (2%)
    all_to_all x1, waiting for transfers between devices, local_blocks(): lax.all_to_all(packed, 'graph', split_axis=0, concat_axis=0, tiled=True)  9.66 us
    all_to_all x1, starting transfers between devices, local_blocks(): lax.all_to_all(packed, 'graph', split_axis=0, concat_axis=0, tiled=True)  7.36 us
    pallas_call x1, Pallas kernels, local_blocks(): pl.pallas_call(main_kernel, in_specs=[near] * 11 + [far] * 2, out_shape=(...  7.32 us
    pallas_call x1, Pallas kernels, local_blocks(): pl.pallas_call(ahead_kernel, in_specs=[far] * 12, out_specs=[near] * 10,...  2.01 us
    pallas_call x1, Pallas kernels, local_blocks(): pl.pallas_call(pack_kernel, out_shape=jax.ShapeDtypeStruct((peers, rows,...  1.93 us
  transfers between devices with their start and end apart: 1, of which 1 were waited for; matrix products, arithmetic and copies ran while one was open for 0% of the time, Pallas kernels for 7%

profile of v8, /device:TPU:0, one launch (start us, length us, event | category | flops | bytes accessed | tf_op | source)
XLA Modules:
  0.0 28.9 jit_solution(4322043720680598535)
XLA Ops:
  0.6 1.9 %pack.1 = bf16[16,88,128]{2,1,0:T(8,128)(2,1)} custom-call(bf16[16,8192]{1,0:T(8,128)(2,1)} %basis_ref.1, s32[64,128]{1,0:T(8,128)} %bitcast.12, s32[64,128]{1,0:T(8,128)} %bitcast.13, s32[64,128]{1,0:T(8,128)} %bitcast.14, bf16[16,256]{1,0:T(8,128)(2,1)} %atom_far.1, s32[1,128]{1,0:T(1,128)} %bitcast.17), custom_call_target="tpu_custom_call" | custom-call | tf_op jit(solution)/shard_map/pack/pallas_call | solution.py:327
  2.6 7.4 %all-to-all-start = ((bf16[16,88,128]{2,1,0:T(8,128)(2,1)}), bf16[16,88,128]{2,1,0:T(8,128)(2,1)S(1)}, u32[]{:S(2)}, u32[]{:S(2)}) async-start(bf16[16,88,128]{2,1,0:T(8,128)(2,1)} %pack.1), calls=%async_computation | async-start | bytes 720896 | tf_op jit(solution)/shard_map/all_to_all | solution.py:339
  9.9 2.0 %ahead.1 = (bf16[256,512]{1,0:T(8,128)(2,1)S(1)}, f32[256,512]{1,0:T(8,128)S(1)}, bf16[256,128]{1,0:T(8,128)(2,1)S(1)}, bf16[64,640]{1,0:T(8,128)(2,1)S(1)}, bf1...) custom-call(bf16[256,512]{1,0:T(8,128)(2,1)} %edge_far.1, ...), custom_call_target="tpu_custom_call" | custom-call | tf_op jit(solution)/shard_map/ahead/pallas_call | solution.py:352
  11.9 9.7 %all-to-all-done.recv_ref = bf16[16,88,128]{2,1,0:T(8,128)(2,1)S(1)} async-done(((bf16[16,88,128]{2,1,0:T(8,128)(2,1)}), bf16[16,88,128]{2,1,0:T(8,128)(2,1)S(1)}, u32[]{:S(2)}, u32[]{:S(2)}) %all-to-all-start) | async-done | bytes 360480 | tf_op jit(solution)/shard_map/all_to_all | solution.py:339
  21.6 7.3 %block.1 = (bf16[256,512]{1,0:T(8,128)(2,1)}, bf16[16,256]{1,0:T(8,128)(2,1)}) custom-call(bf16[16,88,128]{2,1,0:T(8,128)(2,1)S(1)} %all-to-all-done.recv_ref, bf16[256,512]{1,0:T(8,128)(2,1)S(1)} %get-tuple-element.12.edge_ref, f32[256,512]{1,0:T(8,128)S(1)} %get-tuple-element.13.pre_ref, bf16[256,128]{1,0:T(8,128)(2,1)S(1)} %get-tuple-element.14.source_hot_ref, ...), custom_call_target="tpu_custom_call" | custom-call | tf_op jit(solution)/shard_map/block/pallas_call | solution.py:392
Async XLA Ops:
  2.6 19.0 %all-to-all-start = ((bf16[16,88,128]{2,1,0:T(8,128)(2,1)}), bf16[16,88,128]{2,1,0:T(8,128)(2,1)S(1)}, u32[]{:S(2)}, u32[]{:S(2)}) async-start(bf16[16,88,128]{2,1,0:T(8,128)(2,1)} %pack.1), calls=%async_computation | async-start | bytes 720896 | tf_op jit(solution)/shard_map/all_to_all | solution.py:339
